TPU v7x, 256 devices: a whole 4x4x8 slice. The times are simulated.
256 devices in a mesh: seq: 32 (over x, y, core), help: 8 (over z).
Axes of the slice: x: 4, y: 4, z: 8, core: 2. Of those that a mesh axis runs over, the one named last changes fastest.
Arguments:
- queries: bfloat16 [16384, 4096], P('seq'), may hold values from -7 to 7
- keys_values: bfloat16 [16384, 2048], P('seq'), may hold values from -10 to 10
- verticals: int32 [32, 24], P('seq'), may hold values from 0 to 255, as said below
- slashes: int32 [32, 24], P('seq'), may hold values from 0 to 255, as said below
- units: int32 [32, 8, 192], P('seq', 'help'), may hold values from -1 to 1535, as said below
Outputs:
- attended: bfloat16 [16384, 4096], P(('seq', 'help'))
Inputs may be any that keep to these rules, and one draw needn't show every extreme that they name: `verticals`: each head's 24 key tiles are distinct and ascending and include tile 0 and tile 256 - 1. `slashes`: each head's 24 offsets are distinct and ascending and include 0 and 255. Each list holds codes i * 6 + c in ascending order followed by -1 entries; a head's codes, each once, are units with an attended slot, among them the unit of the slot of slash offset 0 for every tile i; for some helper r, the head's lists of helpers r, r + 1, ... taken cyclically and joined in that order hold all its codes in ascending order, every list before the last nonempty one in that order holds 192 codes, and the lists after it are empty.
All inputs are finite; a program needn't handle non-finite values.
Results may differ from a plain program's by a relative error of at most 0.0042.
Values may be sent and summed in bfloat16 or wider, within the bound.
A program may use at most 128 MiB of HBM per device.

v0:
```python
import jax
import jax.numpy as jnp
from jax import lax
from jax.sharding import PartitionSpec as P

HEADS = 32
KV_HEADS = 8
HEAD_DIM = 128
TILE = 64


NEG_FILL = -1e30


def slot_tiles(tile_rows, group_ids, vert_row, slash_row, group_size):
    nvert = vert_row.shape[0]
    slot_pos = group_ids[:, None] * group_size + jnp.arange(group_size, dtype=jnp.int32)[None, :]
    slot_table = jnp.concatenate([vert_row, slash_row])
    match_mask = slot_pos[..., None] == jnp.arange(2 * nvert, dtype=jnp.int32)[None, None, :]
    picked = jnp.sum(jnp.where(match_mask, slot_table[None, None, :], 0), axis=-1)
    is_vert = slot_pos < nvert
    row_tiles = tile_rows[:, None]
    covered = jnp.any((row_tiles - picked)[..., None] == slash_row[None, None, :], axis=-1)
    key_tile = jnp.where(is_vert, picked, row_tiles - picked)
    attended = jnp.where(
        is_vert, (picked <= row_tiles) & jnp.logical_not(covered), picked <= row_tiles
    )
    return (key_tile, attended)


def unit_partials(query_tiles, kv_tiles, tile_rows, group_ids, vert_row, slash_row, group_size):
    head_dim = query_tiles.shape[2]
    key_tile, attended = slot_tiles(tile_rows, group_ids, vert_row, slash_row, group_size)
    safe_tile = jnp.clip(key_tile, 0, kv_tiles.shape[0] - 1)
    kv_picked = jnp.take(kv_tiles, safe_tile, axis=0)
    q_picked = jnp.take(query_tiles, tile_rows, axis=0)
    scores = jnp.einsum(
        "uqd,ugkd->uqgk", q_picked, kv_picked[..., :head_dim], preferred_element_type=jnp.float32
    ) * head_dim ** (-0.5)
    tile_len = query_tiles.shape[1]
    lower_mask = jnp.arange(tile_len)[None, :] <= jnp.arange(tile_len)[:, None]
    near_tile = (key_tile < tile_rows[:, None])[:, None, :, None]
    allowed = attended[:, None, :, None] & (near_tile | lower_mask[None, :, None, :])
    masked = jnp.where(allowed, scores, NEG_FILL)
    row_max = jnp.max(masked, axis=(2, 3))
    exp_terms = jnp.exp(masked - row_max[:, :, None, None])
    row_sum = jnp.sum(exp_terms, axis=(2, 3))
    weights = exp_terms.astype(jnp.bfloat16)
    outputs = jnp.einsum(
        "uqgk,ugkd->uqd", weights, kv_picked[..., head_dim:], preferred_element_type=jnp.float32
    )
    return (row_max, row_sum, outputs)


def head_partials(code_list, query_tiles, kv_tiles, vert_row, slash_row):
    n_tiles, tile_len, head_dim = query_tiles.shape
    nvert = vert_row.shape[0]
    group_size = min(8, nvert)
    n_groups = 2 * nvert // group_size
    step_units = min(32, code_list.shape[0])
    unit_count = jnp.sum((code_list >= 0).astype(jnp.int32))
    n_steps = (unit_count + step_units - 1) // step_units
    state_init = (
        jnp.array(-1, jnp.int32),
        jnp.full((tile_len,), NEG_FILL, jnp.float32),
        jnp.zeros((tile_len,), jnp.float32),
        jnp.zeros((tile_len, head_dim), jnp.float32),
        jnp.zeros((n_tiles, tile_len, head_dim), jnp.float32),
        jnp.full((n_tiles, tile_len), NEG_FILL, jnp.float32),
        jnp.zeros((n_tiles, tile_len), jnp.float32),
    )

    def advance(block_pos, state_all):
        current, run_max, run_sum, run_acc, acc_all, max_all, sum_all = state_all
        block_codes = lax.dynamic_slice_in_dim(code_list, block_pos * step_units, step_units)
        active = block_codes >= 0
        safe_code = jnp.maximum(block_codes, 0)
        tile_rows = safe_code // n_groups
        group_ids = safe_code % n_groups
        row_max, row_sum, outputs = unit_partials(
            query_tiles, kv_tiles, tile_rows, group_ids, vert_row, slash_row, group_size
        )
        for unit_pos in range(step_units):
            tile_now = tile_rows[unit_pos]
            same_tile = tile_now == current
            new_max = jnp.where(
                same_tile, jnp.maximum(run_max, row_max[unit_pos]), row_max[unit_pos]
            )
            keep_old = jnp.where(same_tile, jnp.exp(run_max - new_max), 0.0)
            fresh_scale = jnp.exp(row_max[unit_pos] - new_max)
            new_sum = run_sum * keep_old + row_sum[unit_pos] * fresh_scale
            new_acc = run_acc * keep_old[:, None] + outputs[unit_pos] * fresh_scale[:, None]
            is_live = active[unit_pos]
            current = jnp.where(is_live, tile_now, current)
            run_max = jnp.where(is_live, new_max, run_max)
            run_sum = jnp.where(is_live, new_sum, run_sum)
            run_acc = jnp.where(is_live, new_acc, run_acc)
            acc_all = lax.dynamic_update_slice(acc_all, run_acc[None], (current, 0, 0))
            max_all = lax.dynamic_update_slice(max_all, run_max[None], (current, 0))
            sum_all = lax.dynamic_update_slice(sum_all, run_sum[None], (current, 0))
        return (current, run_max, run_sum, run_acc, acc_all, max_all, sum_all)

    state_all = lax.fori_loop(0, n_steps, advance, state_init)
    return (state_all[4], state_all[5], state_all[6])


def per_device(queries, keys_values, verticals, slashes, units):
    seq_count = lax.axis_size("seq")
    help_count = lax.axis_size("help")
    local_rows = queries.shape[0]
    heads_local = HEADS // seq_count
    head_dim = HEAD_DIM
    group_heads = HEADS // KV_HEADS
    token_count = local_rows * seq_count
    n_tiles = token_count // TILE
    query_cube = queries.reshape(local_rows, HEADS, head_dim)
    kv_split = keys_values.reshape(local_rows, 2, KV_HEADS, head_dim)
    kv_joined = jnp.concatenate([kv_split[:, 0], kv_split[:, 1]], axis=-1)
    kv_spread = jnp.broadcast_to(
        kv_joined[:, :, None, :], (local_rows, KV_HEADS, group_heads, 2 * head_dim)
    )
    kv_spread = kv_spread.reshape(local_rows, HEADS, 2 * head_dim)
    head_queries, head_kv = (
        lax.all_to_all(query_cube, "seq", split_axis=1, concat_axis=0, tiled=True),
        lax.all_to_all(kv_spread, "seq", split_axis=1, concat_axis=0, tiled=True),
    )
    kv_lookup = head_kv[:, 0]
    plan_lists = units[0, 0]
    query_tiles = head_queries[:, 0].reshape(n_tiles, TILE, head_dim)
    kv_tiles = kv_lookup.reshape(n_tiles, TILE, 2 * head_dim)
    acc_all, max_all, sum_all = head_partials(
        plan_lists, query_tiles, kv_tiles, verticals[0], slashes[0]
    )
    acc_parts = [acc_all]
    max_parts = [max_all]
    sum_parts = [sum_all]
    out_rows = local_rows // help_count
    acc_send = jnp.stack(acc_parts).reshape(heads_local, seq_count, help_count, out_rows, head_dim)
    max_send = jnp.stack(max_parts).reshape(heads_local, seq_count, help_count, out_rows)
    sum_send = jnp.stack(sum_parts).reshape(heads_local, seq_count, help_count, out_rows)
    got_acc, got_max, got_sum = (
        lax.all_to_all(acc_send, "help", split_axis=2, concat_axis=2, tiled=True),
        lax.all_to_all(max_send, "help", split_axis=2, concat_axis=2, tiled=True),
        lax.all_to_all(sum_send, "help", split_axis=2, concat_axis=2, tiled=True),
    )
    top_max = jnp.max(got_max, axis=2, keepdims=True)
    scale_w = jnp.exp(got_max - top_max)
    numerator = jnp.sum(got_acc * scale_w[..., None], axis=2)
    denominator = jnp.sum(got_sum * scale_w, axis=2)
    head_out = (numerator / denominator[..., None]).astype(jnp.bfloat16)
    arranged = jnp.transpose(head_out, (2, 1, 0, 3))
    returned = lax.all_to_all(arranged, "seq", split_axis=1, concat_axis=2, tiled=True)
    return returned.reshape(out_rows, HEADS * head_dim)


def solution(mesh):
    in_specs = (
        P("seq", None),
        P("seq", None),
        P("seq", None),
        P("seq", None),
        P("seq", "help", None),
    )
    out_specs = P(("seq", "help"), None)
    return jax.shard_map(
        per_device, mesh=mesh, in_specs=in_specs, out_specs=out_specs, check_vma=False
    )
```

profile of v0, /device:TPU:7, one launch (start us, length us, event | category | flops | bytes accessed | tf_op | source)
XLA Modules:
  0.0 1489.0 jit_solution(8066338086374980907)
XLA Ops:
  0.0 5.4 copy_bitcast_fusion
  5.5 8.0 all-to-all-start
  13.4 0.6 copy.52
  14.5 0.4 copy.37
  14.9 49.2 %all-to-all-done = bf16[512,32,128]{2,0,1:T(8,128)(2,1)} async-done(((bf16[512,32,128]{2,0,1:T(8,128)(2,1)}), bf16[512,32,128]{2,0,1:T(8,128)(2,1)}, u32[]{:S(2)}, u32[]{:S(2)}) %all-to-all-start) | async-done | bytes 4194336 | tf_op jit(solution)/shard_map/all_to_all | solution.py:124
  64.1 4.2 broadcast_in_dim.787
  68.3 8.9 all-to-all-start.1
  77.2 0.7 fusion.191
  78.6 102.4 %all-to-all-done.1 = bf16[512,32,256]{2,0,1:T(8,128)(2,1)} async-done(((bf16[512,32,256]{2,0,1:T(8,128)(2,1)}), bf16[512,32,256]{2,0,1:T(8,128)(2,1)}, u32[]{:S(2)}, u32[]{:S(2)}) %all-to-all-start.1) | async-done | bytes 8388640 | tf_op jit(solution)/shard_map/all_to_all | solution.py:125
  181.0 4.3 broadcast_in_dim.784
  185.3 0.8 reshape.380
  186.1 1050.0 %all-to-all-start.4 = ((f32[8,1,2048]{2,1,0:T(1,128)}), f32[8,1,2048]{2,1,0:T(1,128)S(1)}, u32[]{:S(2)}, u32[]{:S(2)}) async-start(f32[8,1,2048]{2,1,0:T(1,128)} %reshape.380), calls=%async_computation.4 | async-start | bytes 131072 | tf_op jit(solution)/shard_map/all_to_all | solution.py:144
  1236.1 0.8 reshape.382
  1236.9 6.4 all-to-all-done.4
  1243.3 3.4 all-to-all-start.3
  1246.7 8.3 copy.38
  1255.0 6.6 all-to-all-start.2
  1261.5 0.5 broadcast.433
  1262.0 0.8 reduce.3
  1262.9 0.8 reduce.4
  1263.9 184.8 %all-to-all-done.2 = f32[1,32,8,64,128]{4,3,1,0,2:T(8,128)} async-done(((f32[1,32,8,64,128]{4,3,1,0,2:T(8,128)}), f32[1,32,8,64,128]{4,3,1,0,2:T(8,128)}, u32[]{:S(2)}, u32[]{:S(2)}) %all-to-all-start.2) | async-done | bytes 8388640 | tf_op jit(solution)/shard_map/all_to_all | solution.py:142
  1448.7 5.3 multiply_reduce_fusion
  1454.4 33.3 %all_to_all.54 = bf16[64,32,1,128]{3,0,2,1:T(8,128)(2,1)S(1)} all-to-all(bf16[64,32,1,128]{3,0,2,1:T(8,128)(2,1)S(1)} %fusion.189), channel_id=1, replica_groups=mesh['seq'=32,'help'=8] {'seq'}, dimensions={1} | all-to-all | bytes 1048576 | tf_op jit(solution)/shard_map/all_to_all | solution.py:152
  1488.0 1.0 copy.58
  (26 shorter events, 1.5 us)
Async XLA Ops:
  0.0 13.4 copy-start.1
  5.5 58.6 %all-to-all-start = ((bf16[512,32,128]{2,0,1:T(8,128)(2,1)}), bf16[512,32,128]{2,0,1:T(8,128)(2,1)}, u32[]{:S(2)}, u32[]{:S(2)}) async-start(bf16[512,32,128]{2,0,1:T(8,128)(2,1)} %copy_bitcast_fusion), calls=%async_computation | async-start | bytes 8388608 | tf_op jit(solution)/shard_map/all_to_all | solution.py:124
  68.2 8.9 copy-start.2
  68.2 10.2 copy-start.3
  68.3 10.2 copy-start.4
  68.3 112.7 %all-to-all-start.1 = ((bf16[512,32,256]{2,0,1:T(8,128)(2,1)}), bf16[512,32,256]{2,0,1:T(8,128)(2,1)}, u32[]{:S(2)}, u32[]{:S(2)}) async-start(bf16[512,32,256]{2,0,1:T(8,128)(2,1)} %bitcast.1753), calls=%async_computation.1 | async-start | bytes 16777216 | tf_op jit(solution)/shard_map/all_to_all | solution.py:125
  186.1 1057.2 %all-to-all-start.4 = ((f32[8,1,2048]{2,1,0:T(1,128)}), f32[8,1,2048]{2,1,0:T(1,128)S(1)}, u32[]{:S(2)}, u32[]{:S(2)}) async-start(f32[8,1,2048]{2,1,0:T(1,128)} %reshape.380), calls=%async_computation.4 | async-start | bytes 131072 | tf_op jit(solution)/shard_map/all_to_all | solution.py:144
  1243.3 11.6 all-to-all-start.3
  1255.0 193.7 %all-to-all-start.2 = ((f32[1,32,8,64,128]{4,3,1,0,2:T(8,128)}), f32[1,32,8,64,128]{4,3,1,0,2:T(8,128)}, u32[]{:S(2)}, u32[]{:S(2)}) async-start(f32[1,32,8,64,128]{4,3,1,0,2:T(8,128)} %copy.38), calls=%async_computation.2 | async-start | bytes 16777216 | tf_op jit(solution)/shard_map/all_to_all | solution.py:142
where the time goes:
time: 1500 us; the launch traced here: 1490 us
  starting transfers between devices  1080 us (72%)
  waiting for transfers between devices  343 us (23%)
  blocking collectives  33.3 us (2%)
  local copies, waits for them, and re-layouts  27 us (2%)
    all_to_all x1, starting transfers between devices, per_device(): lax.all_to_all(sum_send, 'help', split_axis=2, concat_axis=2, tiled=True)  1050 us
    all_to_all x1, waiting for transfers between devices, per_device(): lax.all_to_all(acc_send, 'help', split_axis=2, concat_axis=2, tiled=True)  185 us
    all_to_all x1, waiting for transfers between devices, per_device(): lax.all_to_all(kv_spread, 'seq', split_axis=1, concat_axis=0, tiled=True)  102 us
    all_to_all x1, waiting for transfers between devices, per_device(): lax.all_to_all(query_cube, 'seq', split_axis=1, concat_axis=0, tiled=True)  49.2 us
    all_to_all x1, blocking collectives, per_device(): lax.all_to_all(arranged, 'seq', split_axis=1, concat_axis=2, tiled=True)  33.3 us
  transfers between devices with their start and end apart: 5, of which 4 were waited for; matrix products, arithmetic and copies ran while one was open for 1% of the time, Pallas kernels for 0%

commit v1 on v0

v1 whole, which is shorter than its diff:
```python
import functools

import jax
import jax.numpy as jnp
from jax import lax
from jax.experimental import pallas as pl
from jax.experimental.pallas import tpu as pltpu
from jax.sharding import PartitionSpec as P

HEADS = 32
KV_HEADS = 8
HEAD_DIM = 128
TILE = 64
NVERT = 24
NGROUP = 6
GROUP_HEADS = 4
TILES_LOCAL = 8
KEYS = NVERT * TILE
CHUNK = 256
CHUNK_TILES = CHUNK // TILE
NCHUNK = KEYS // CHUNK
ROWS = TILES_LOCAL * TILE
NEG = -1e30
EXP_SCALE = HEAD_DIM ** -0.5 * 1.4426950408889634


def dot_t(a, b):
    return lax.dot_general(a, b, (((1,), (1,)), ((), ())), preferred_element_type=jnp.float32)


def make_bias(first_tile, lists, vs_ref, bias_v, bias_s):
    lane = lax.broadcasted_iota(jnp.int32, (TILES_LOCAL, 128), 1)
    tile = lax.broadcasted_iota(jnp.int32, (TILES_LOCAL, 128), 0) + first_tile
    slot_of = lax.broadcasted_iota(jnp.int32, (128, KEYS), 1) // TILE
    spread = jnp.where(slot_of == lax.broadcasted_iota(jnp.int32, (128, KEYS), 0), 1.0, 0.0).astype(jnp.bfloat16)
    width = lists.shape[-1]
    row_tile = lax.broadcasted_iota(jnp.int32, (TILES_LOCAL, width), 0) + first_tile
    for k in range(GROUP_HEADS):
        total = jnp.zeros((TILES_LOCAL, width), jnp.int32)
        for r in range(lists.shape[1]):
            code = jnp.broadcast_to(lists[k, r:r + 1, :], (TILES_LOCAL, width))
            group = code - row_tile * NGROUP
            total += jnp.where((group >= 0) & (group < NGROUP), lax.shift_left(1, jnp.clip(group, 0, NGROUP - 1)), 0)
        named = jnp.sum(total, axis=1, keepdims=True)
        vert = jnp.broadcast_to(vs_ref[k:k + 1, :], (TILES_LOCAL, 128))
        slash = jnp.broadcast_to(vs_ref[GROUP_HEADS + k:GROUP_HEADS + k + 1, :], (TILES_LOCAL, 128))
        covered = jnp.zeros((TILES_LOCAL, 128), jnp.bool_)
        for n in range(NVERT):
            covered |= (tile - vert) == slash[:, n:n + 1]
        unit = lane // 8
        bit_v = lax.shift_right_logical(jnp.broadcast_to(named, unit.shape), jnp.minimum(unit, 2)) & 1
        bit_s = lax.shift_right_logical(jnp.broadcast_to(named, unit.shape), jnp.minimum(unit + 3, 5)) & 1
        real = lane < NVERT
        att_v = real & (vert <= tile) & jnp.logical_not(covered) & (bit_v == 1)
        att_s = real & (slash <= tile) & (bit_s == 1)
        for att, bias in ((att_v, bias_v), (att_s, bias_s)):
            hot = jnp.where(att, 1.0, 0.0).astype(jnp.bfloat16)
            wide = jnp.dot(hot, spread, preferred_element_type=jnp.float32)
            bias[k] = ((wide - 1.0) * (-NEG)).reshape(TILES_LOCAL, 1, KEYS)


def tiles_of(ref, places):
    return jnp.concatenate([ref[pl.ds(pl.multiple_of(p * TILE, TILE), TILE), :] for p in places], axis=0)


def score_head(k, first_tile, q_ref, k_ref, verts, slashes, bias_v, bias_s, score_v, p_v, p_s, ell):
    q_cols = pl.ds(pl.multiple_of(k * HEAD_DIM, HEAD_DIM), HEAD_DIM)
    for c in range(NCHUNK):
        keys = tiles_of(k_ref, [verts[k, c * CHUNK_TILES + n] for n in range(CHUNK_TILES)])
        s = dot_t(q_ref[:, q_cols], keys)
        cols = slice(c * CHUNK, (c + 1) * CHUNK)
        s = s.reshape(TILES_LOCAL, TILE, CHUNK) + bias_v[k, :, :, cols]
        score_v[:, cols] = s.reshape(ROWS, CHUNK)
    row = lax.broadcasted_iota(jnp.int32, (TILE, CHUNK), 0)
    col = lax.broadcasted_iota(jnp.int32, (TILE, CHUNK), 1)
    diagonal = jnp.where((col < TILE) & (col > row), NEG, 0.0)

    @pl.loop(0, TILES_LOCAL)
    def _(t):
        rows = pl.ds(pl.multiple_of(t * TILE, TILE), TILE)
        q = q_ref[rows, q_cols]
        parts = []
        for c in range(NCHUNK):
            places = [jnp.maximum(first_tile + t - slashes[k, c * CHUNK_TILES + n], 0) for n in range(CHUNK_TILES)]
            s = dot_t(q, tiles_of(k_ref, places))
            s = s + bias_s[k, t, :, c * CHUNK:(c + 1) * CHUNK]
            if c == 0:
                s = s + diagonal
            parts.append(s)
        for c in range(NCHUNK):
            parts.append(score_v[rows, c * CHUNK:(c + 1) * CHUNK])
        peak = functools.reduce(jnp.maximum, parts)
        peak = jnp.max(peak, axis=1, keepdims=True)
        total = jnp.zeros((TILE, CHUNK), jnp.float32)
        for c, s in enumerate(parts):
            p = jnp.exp2((s - peak) * EXP_SCALE)
            total += p
            out = p_s if c < NCHUNK else p_v
            cc = c % NCHUNK
            out[k, rows, cc * CHUNK:(cc + 1) * CHUNK] = p.astype(jnp.bfloat16)
        ell[k, rows, :] = jnp.broadcast_to(jnp.sum(total, axis=1, keepdims=True), (TILE, HEAD_DIM))


def value_head(k, first_tile, v_ref, verts, slashes, p_v, p_s, ell, acc, out_ref):
    values = tiles_of(v_ref, [verts[k, n] for n in range(NVERT)])
    acc[...] = jnp.dot(p_v[k], values, preferred_element_type=jnp.float32)
    out_cols = pl.ds(pl.multiple_of(k * HEAD_DIM, HEAD_DIM), HEAD_DIM)

    @pl.loop(0, TILES_LOCAL)
    def _(t):
        rows = pl.ds(pl.multiple_of(t * TILE, TILE), TILE)
        places = [jnp.maximum(first_tile + t - slashes[k, n], 0) for n in range(NVERT)]
        o = jnp.dot(p_s[k, rows, :], tiles_of(v_ref, places), preferred_element_type=jnp.float32)
        out_ref[rows, out_cols] = ((o + acc[rows, :]) / ell[k, rows, :]).astype(jnp.bfloat16)


def attend_kernel(first_ref, verts, slashes, vs_ref, lists, q_ref, k_ref, v_ref, out_ref,
                  bias_v, bias_s, score_v, p_v, p_s, ell, acc):
    first_tile = first_ref[0]
    make_bias(first_tile, lists, vs_ref, bias_v, bias_s)

    @pl.loop(0, GROUP_HEADS)
    def _(k):
        score_head(k, first_tile, q_ref, k_ref, verts, slashes, bias_v, bias_s, score_v, p_v, p_s, ell)

    @pl.loop(0, GROUP_HEADS)
    def _(k):
        value_head(k, first_tile, v_ref, verts, slashes, p_v, p_s, ell, acc, out_ref)


def scratch():
    return [
        pltpu.VMEM((GROUP_HEADS, TILES_LOCAL, 1, KEYS), jnp.float32),
        pltpu.VMEM((GROUP_HEADS, TILES_LOCAL, 1, KEYS), jnp.float32),
        pltpu.VMEM((ROWS, KEYS), jnp.float32),
        pltpu.VMEM((GROUP_HEADS, ROWS, KEYS), jnp.bfloat16),
        pltpu.VMEM((GROUP_HEADS, ROWS, KEYS), jnp.bfloat16),
        pltpu.VMEM((GROUP_HEADS, ROWS, HEAD_DIM), jnp.float32),
        pltpu.VMEM((ROWS, HEAD_DIM), jnp.float32),
    ]


def attend(first, verts, slashes, vs, lists, q, keys, values):
    smem = pl.BlockSpec(memory_space=pltpu.SMEM)
    vmem = pl.BlockSpec(memory_space=pltpu.VMEM)
    return pl.pallas_call(
        attend_kernel,
        out_shape=jax.ShapeDtypeStruct((ROWS, GROUP_HEADS * HEAD_DIM), jnp.bfloat16),
        in_specs=[smem, smem, smem, vmem, vmem, vmem, vmem, vmem],
        out_specs=vmem,
        scratch_shapes=scratch(),
        compiler_params=pltpu.CompilerParams(vmem_limit_bytes=56 * 1024 * 1024),
        name="attend",
    )(first, verts, slashes, vs, lists, q, keys, values)


def per_device(queries, keys_values, verticals, slashes, units):
    s = lax.axis_index("seq")
    z = lax.axis_index("help")
    kv_cols = KV_HEADS * HEAD_DIM
    local_k = lax.dynamic_slice_in_dim(keys_values, z * HEAD_DIM, HEAD_DIM, 1)
    local_v = lax.dynamic_slice_in_dim(keys_values, kv_cols + z * HEAD_DIM, HEAD_DIM, 1)
    q = lax.dynamic_slice_in_dim(queries, z * GROUP_HEADS * HEAD_DIM, GROUP_HEADS * HEAD_DIM, 1)
    lists = lax.all_gather(units[0, 0], "help", axis=0)
    plan = jnp.concatenate([lists.reshape(-1), verticals[0], slashes[0]])
    plan = lax.all_gather(plan, "seq", axis=0)
    plan = lax.dynamic_slice_in_dim(plan, z * GROUP_HEADS, GROUP_HEADS, 0)
    n_list = lists.size
    lists = plan[:, :n_list].reshape((GROUP_HEADS,) + lists.shape)
    verts = plan[:, n_list:n_list + NVERT]
    slash = plan[:, n_list + NVERT:]
    vs = jnp.pad(jnp.concatenate([verts, slash]), ((0, 0), (0, 128 - NVERT)))
    keys = lax.all_gather(local_k, "seq", axis=0, tiled=True)
    values = lax.all_gather(local_v, "seq", axis=0, tiled=True)
    first = jnp.full((1,), s * TILES_LOCAL, jnp.int32)
    out = attend(first, verts, slash, vs, lists, q, keys, values)
    return lax.all_to_all(out, "help", split_axis=0, concat_axis=1, tiled=True)


def solution(mesh):
    in_specs = (
        P("seq", None),
        P("seq", None),
        P("seq", None),
        P("seq", None),
        P("seq", "help", None),
    )
    out_specs = P(("seq", "help"), None)
    return jax.shard_map(
        per_device, mesh=mesh, in_specs=in_specs, out_specs=out_specs, check_vma=False
    )
```

time: 1500 us -> 312 us (0.21)
  starting transfers between devices: 1080 us -> 0.09 us
  waiting for transfers between devices: 343 us -> 212 us
  Pallas kernels: 0 us -> 33.6 us
  local copies, waits for them, and re-layouts: 27 us -> 10.6 us
    all_to_all x5 -> x0, starting transfers between devices: 1080 us -> none  [the longest x1 1050 us: per_device(): lax.all_to_all(sum_send, 'help', split_axis=2, concat_axis=2, tiled=True)]
    all_to_all x5 -> x0, waiting for transfers between devices: 343 us -> none  [the longest x1 185 us: per_device(): lax.all_to_all(acc_send, 'help', split_axis=2, concat_axis=2, tiled=True)]
    unnamed x0 -> x4, waiting for transfers between devices: none -> 107 us
    all_gather x0 -> x2, waiting for transfers between devices: none -> 105 us  [the longest x1 53.4 us: per_device(): keys = lax.all_gather(local_k, 'seq', axis=0, tiled=True)]
    pallas_call x0 -> x1, Pallas kernels: none -> 33.6 us  [attend(): pl.pallas_call(attend_kernel, out_shape=jax.ShapeDtypeStruct((ROWS, GROUP...]
    all_gather x0 -> x1, blocking collectives: none -> 15.9 us  [per_device(): lists = lax.all_gather(units[0, 0], 'help', axis=0)]
  transfers between devices with their start and end apart: 5 -> 3, of which waited for: 4 -> 3; matrix products, arithmetic and copies ran while one was open for 1% -> 2% of each run, Pallas kernels for 0% -> 0%
where the time goes in v1:
time: 312 us; the launch traced here: 310 us
  waiting for transfers between devices  212 us (68%)
  blocking collectives  40 us (13%)
  Pallas kernels  33.6 us (11%)
  between operations  13.8 us (4%)
  local copies, waits for them, and re-layouts  10.6 us (3%)
    unnamed x4, waiting for transfers between devices  107 us
    all_gather x1, waiting for transfers between devices, per_device(): keys = lax.all_gather(local_k, 'seq', axis=0, tiled=True)  53.4 us
    all_gather x1, waiting for transfers between devices, per_device(): values = lax.all_gather(local_v, 'seq', axis=0, tiled=True)  51.2 us
    pallas_call x1, Pallas kernels, attend(): pl.pallas_call(attend_kernel, out_shape=jax.ShapeDtypeStruct((ROWS, GROUP...  33.6 us
    all_to_all x1, blocking collectives, per_device(): return lax.all_to_all(out, 'help', split_axis=0, concat_axis=1, tiled=True)  24.1 us
    all_gather x1, blocking collectives, per_device(): lists = lax.all_gather(units[0, 0], 'help', axis=0)  15.9 us
  transfers between devices with their start and end apart: 3, of which 3 were waited for; matrix products, arithmetic and copies ran while one was open for 2% of the time, Pallas kernels for 0%

profile of v1, /device:TPU:7, one launch (start us, length us, event | category | flops | bytes accessed | tf_op | source)
XLA Modules:
  0.0 310.2 jit_solution(1161515014521082036)
XLA Ops:
  6.5 0.0 all-reduce.5.cloned.1.call-start
  6.5 15.9 %all-gather = s32[8,1,192]{2,1,0:T(1,128)S(1)} all-gather(s32[1,1,192]{2,1,0:T(1,128)} %param.9), channel_id=2, replica_groups=mesh['seq'=32,'help'=8] {'help'}, dimensions={0}, use_global_device_ids=true | all-gather | bytes 6912 | tf_op jit(solution)/shard_map/all_gather | solution.py:164
  22.4 0.1 reshape.9
  22.5 1.3 dynamic-slice
  24.4 0.7 concatenate.6
  25.2 0.3 dynamic-update-slice
  25.5 0.9 reshape.12
  26.4 0.0 all-reduce.5.cloned.1.call-update
  26.4 0.0 all-gather.7.cloned.1.call-start
  26.4 1.7 constant_dynamic-slice_fusion
  28.1 0.0 all-gather.7.cloned.1.call-update
  28.2 0.0 all-gather.5.cloned.1.call-start
  28.2 0.7 all-gather.5.cloned.1.call-update
  28.9 1.9 constant_dynamic-slice_fusion.2.q_ref
  30.8 106.7 %all-reduce.5.cloned.1.call-done = s32[32,1584]{1,0:T(8,128)} async-done(((s32[32,1584]{1,0:T(8,128)}), s32[32,1584]{1,0:T(8,128)}) %all-reduce.5.cloned.1.call-update) | async-done | bytes 202768
  137.5 0.8 fusion
  138.4 0.6 pad.4.vs_ref
  138.9 0.8 constant_dynamic-slice_fusion.3
  139.8 0.7 reshape.10.lists
  140.4 51.2 %all-gather.7.cloned.1.call-done.v_ref = bf16[16384,128]{1,0:T(8,128)(2,1)} async-done(((bf16[512,128]{1,0:T(8,128)(2,1)}), bf16[16384,128]{1,0:T(8,128)(2,1)}) %all-gather.7.cloned.1.call-update) | async-done | bytes 4194320 | tf_op jit(solution)/shard_map/all_gather | solution.py:174
  191.6 53.4 %all-gather.5.cloned.1.call-done.k_ref = bf16[16384,128]{1,0:T(8,128)(2,1)} async-done(((bf16[512,128]{1,0:T(8,128)(2,1)}), bf16[16384,128]{1,0:T(8,128)(2,1)}) %all-gather.5.cloned.1.call-update) | async-done | bytes 4194320 | tf_op jit(solution)/shard_map/all_gather | solution.py:173
  245.1 33.6 %attend.1 = bf16[512,512]{1,0:T(8,128)(2,1)} custom-call(s32[1]{0:T(128)} %bitcast.first_ref, s32[4,24]{1,0:T(4,128)} %copy-done.1, s32[4,24]{1,0:T(4,128)} %copy-done, s32[8,128]{1,0:T(8,128)} %pad.4.vs_ref, s32[4,8,192]{2,1,0:T(8,128)} %reshape.10.lists, bf16[512,512]{1,0:T(8,128)(2,1)} %constant_dynamic-slice_fusion.2.q_ref, ...), custom_call_target="tpu_custom_call" | custom-call | tf_op jit(solution)/shard_map/attend/pallas_call | solution.py:146
  278.7 24.1 %all_to_all.19 = bf16[8,64,512]{2,1,0:T(8,128)(2,1)S(1)} all-to-all(bf16[8,64,512]{2,1,0:T(8,128)(2,1)} %bitcast.8), channel_id=1, replica_groups=mesh['seq'=32,'help'=8] {'help'}, dimensions={0} | all-to-all | bytes 1048576 | tf_op jit(solution)/shard_map/all_to_all | solution.py:177
  302.8 0.8 copy.8
  (7 shorter events, 0.1 us)
Async XLA Ops:
  6.5 131.0 %all-reduce.5.cloned.1.call-start = ((), (), s32[]{:S(2)}) async-start(), calls=%async_computation.3 | async-start | bytes 425984
  26.4 165.3 %all-gather.7.cloned.1.call-start = ((), (), s32[]{:S(2)}) async-start(), calls=%async_computation.2 | async-start | bytes 4325376 | tf_op jit(solution)/shard_map/all_gather | solution.py:174
  28.2 216.9 %all-gather.5.cloned.1.call-start = ((), (), s32[]{:S(2)}) async-start(), calls=%async_computation.1 | async-start | bytes 4325376 | tf_op jit(solution)/shard_map/all_gather | solution.py:173
  138.3 106.7 %copy-start = (s32[4,24]{1,0:T(4,128)}, s32[4,24]{1,0:T(4,128)S(1)}, u32[]{:S(2)}) copy-start(s32[4,24]{1,0:T(4,128)S(1)} %get-tuple-element.7.slashes) | copy-start | bytes 1156
  138.3 106.7 %copy-start.1 = (s32[4,24]{1,0:T(4,128)}, s32[4,24]{1,0:T(4,128)S(1)}, u32[]{:S(2)}) copy-start(s32[4,24]{1,0:T(4,128)S(1)} %get-tuple-element.8.verts) | copy-start | bytes 1156
Sparse Core Ops, SparseCore 0:
  26.5 110.9 all-reduce.4
  140.4 51.2 all-gather.6
  194.5 50.5 all-gather.4

commit v2 on v1

v2 whole, which is shorter than its diff:
```python
import functools

import jax
import jax.numpy as jnp
from jax import lax
from jax.experimental import pallas as pl
from jax.experimental.pallas import tpu as pltpu
from jax.sharding import PartitionSpec as P

HEADS = 32
KV_HEADS = 8
HEAD_DIM = 128
TILE = 64
NVERT = 24
NGROUP = 6
GROUP_HEADS = 4
TILES_LOCAL = 8
KEYS = NVERT * TILE
CHUNK = 256
CHUNK_TILES = CHUNK // TILE
NCHUNK = KEYS // CHUNK
ROWS = TILES_LOCAL * TILE
NEG = -1e30
HALF = ROWS // 2
MESH = pl.DeviceIdType.MESH
EXP_SCALE = HEAD_DIM ** -0.5 * 1.4426950408889634


def dot_t(a, b):
    return lax.dot_general(a, b, (((1,), (1,)), ((), ())), preferred_element_type=jnp.float32)


def make_bias(first_tile, plan, bias_v, bias_s):
    lane = lax.broadcasted_iota(jnp.int32, (TILES_LOCAL, 128), 1)
    tile = lax.broadcasted_iota(jnp.int32, (TILES_LOCAL, 128), 0) + first_tile
    slot_of = lax.broadcasted_iota(jnp.int32, (128, KEYS), 1) // TILE
    spread = jnp.where(slot_of == lax.broadcasted_iota(jnp.int32, (128, KEYS), 0), 1.0, 0.0).astype(jnp.bfloat16)
    for k in range(GROUP_HEADS):
        named = jnp.zeros((TILES_LOCAL, 128), jnp.int32)
        for n in range(2):
            mask = jnp.broadcast_to(plan[k, n:n + 1, :], (TILES_LOCAL, 128))
            named += jnp.where(lane + n * 128 == tile, mask, 0)
        named = jnp.sum(named, axis=1, keepdims=True)
        vert = jnp.broadcast_to(plan[k, 2:3, :], (TILES_LOCAL, 128))
        slash = jnp.broadcast_to(plan[k, 3:4, :], (TILES_LOCAL, 128))
        covered = jnp.zeros((TILES_LOCAL, 128), jnp.bool_)
        for n in range(NVERT):
            covered |= (tile - vert) == slash[:, n:n + 1]
        unit = lane // 8
        bit_v = lax.shift_right_logical(jnp.broadcast_to(named, unit.shape), jnp.minimum(unit, 2)) & 1
        bit_s = lax.shift_right_logical(jnp.broadcast_to(named, unit.shape), jnp.minimum(unit + 3, 5)) & 1
        real = lane < NVERT
        att_v = real & (vert <= tile) & jnp.logical_not(covered) & (bit_v == 1)
        att_s = real & (slash <= tile) & (bit_s == 1)
        for att, bias in ((att_v, bias_v), (att_s, bias_s)):
            hot = jnp.where(att, 1.0, 0.0).astype(jnp.bfloat16)
            wide = jnp.dot(hot, spread, preferred_element_type=jnp.float32)
            bias[k] = ((wide - 1.0) * (-NEG)).reshape(TILES_LOCAL, 1, KEYS)


def tile_of(ref, place):
    shard = lax.shift_right_logical(place, 3)
    row = (place & (TILES_LOCAL - 1)) * TILE
    return ref[shard, pl.ds(row, TILE), :]


def tiles_of(ref, places):
    return jnp.concatenate([tile_of(ref, p) for p in places], axis=0)


def score_head(k, first_tile, q_ref, k_ref, slots, bias_v, bias_s, score_v, p_v, p_s, ell):
    q_cols = pl.ds(pl.multiple_of(k * HEAD_DIM, HEAD_DIM), HEAD_DIM)
    for c in range(NCHUNK):
        keys = tiles_of(k_ref, [slots[k, 2, c * CHUNK_TILES + n] for n in range(CHUNK_TILES)])
        s = dot_t(q_ref[:, q_cols], keys)
        cols = slice(c * CHUNK, (c + 1) * CHUNK)
        s = s.reshape(TILES_LOCAL, TILE, CHUNK) + bias_v[k, :, :, cols]
        score_v[:, cols] = s.reshape(ROWS, CHUNK)
    row = lax.broadcasted_iota(jnp.int32, (TILE, CHUNK), 0)
    col = lax.broadcasted_iota(jnp.int32, (TILE, CHUNK), 1)
    diagonal = jnp.where((col < TILE) & (col > row), NEG, 0.0)

    @pl.loop(0, TILES_LOCAL)
    def _(t):
        rows = pl.ds(pl.multiple_of(t * TILE, TILE), TILE)
        q = q_ref[rows, q_cols]
        parts = []
        for c in range(NCHUNK):
            places = [jnp.maximum(first_tile + t - slots[k, 3, c * CHUNK_TILES + n], 0) for n in range(CHUNK_TILES)]
            s = dot_t(q, tiles_of(k_ref, places))
            s = s + bias_s[k, t, :, c * CHUNK:(c + 1) * CHUNK]
            if c == 0:
                s = s + diagonal
            parts.append(s)
        for c in range(NCHUNK):
            parts.append(score_v[rows, c * CHUNK:(c + 1) * CHUNK])
        peak = functools.reduce(jnp.maximum, parts)
        peak = jnp.max(peak, axis=1, keepdims=True)
        total = jnp.zeros((TILE, CHUNK), jnp.float32)
        for c, s in enumerate(parts):
            p = jnp.exp2((s - peak) * EXP_SCALE)
            total += p
            out = p_s if c < NCHUNK else p_v
            cc = c % NCHUNK
            out[k, rows, cc * CHUNK:(cc + 1) * CHUNK] = p.astype(jnp.bfloat16)
        ell[k, rows, :] = jnp.broadcast_to(jnp.sum(total, axis=1, keepdims=True), (TILE, HEAD_DIM))


def value_head(k, first_tile, v_ref, slots, p_v, p_s, ell, acc, out_buf):
    values = tiles_of(v_ref, [slots[k, 2, n] for n in range(NVERT)])
    acc[...] = jnp.dot(p_v[k], values, preferred_element_type=jnp.float32)

    @pl.loop(0, TILES_LOCAL)
    def _(t):
        rows = pl.ds(pl.multiple_of(t * TILE, TILE), TILE)
        places = [jnp.maximum(first_tile + t - slots[k, 3, n], 0) for n in range(NVERT)]
        o = jnp.dot(p_s[k, rows, :], tiles_of(v_ref, places), preferred_element_type=jnp.float32)
        out_buf[k, rows, :] = ((o + acc[rows, :]) / ell[k, rows, :]).astype(jnp.bfloat16)


class Gather:
    def __init__(self, me, z, buf, rows, send, recv):
        self.me, self.z, self.buf, self.rows, self.send, self.recv = me, z, buf, rows, send, recv
        self.core = me % 2
        x, y = me // 8, (me // 2) % 4
        c = self.core
        self.a = x * (1 - c) + y * c
        self.b = y * (1 - c) + x * c
        self.started = []

    def at(self, da, db):
        c = self.core
        a, b = (self.a + da) % 4, (self.b + db) % 4
        x = a * (1 - c) + b * c
        y = b * (1 - c) + a * c
        return (x * 4 + y) * 2 + c

    def sibling(self, shard):
        return shard + 1 - 2 * self.core

    def region(self, shard, half):
        if half is None:
            return self.buf.at[shard]
        if half == 0:
            return self.buf.at[shard, pl.ds(0, HALF)]
        return self.buf.at[shard, pl.ds(HALF, self.rows - HALF)]

    def copy(self, shard, half, target, n):
        region = self.region(shard, half)
        return pltpu.make_async_remote_copy(
            src_ref=region, dst_ref=region, send_sem=self.send.at[n],
            recv_sem=self.recv.at[shard, 0 if half is None else half],
            device_id=(target, self.z), device_id_type=MESH)

    def put(self, shard, half, target):
        copy = self.copy(shard, half, target, len(self.started))
        copy.start()
        self.started.append(copy)

    def got(self, shard, half):
        self.copy(shard, half, self.sibling(self.me), 0).wait_recv()

    def put_a(self, shard, half, da):
        self.put(shard, half, self.at(da, 0))

    def put_b(self, shard, half, way=None):
        for db in (1, -1) if way is None else (way,):
            self.put(shard, half, self.at(0, db))

    def across(self, shard):
        self.put(shard, None, self.sibling(self.me))

    def own(self, half):
        mine = self.me
        self.put_a(mine, half, 1)
        self.put_a(mine, half, -1)
        self.put_b(mine, half)

    def first(self):
        left, right = self.at(-1, 0), self.at(1, 0)
        self.got(left, 0)
        self.put_a(left, 0, 1)
        self.got(right, 0)
        self.got(right, 1)
        self.put_a(right, 1, -1)
        self.got(left, 1)
        for shard in (left, right):
            for half in (0, 1):
                self.put_b(shard, half)
            self.across(shard)

    def second(self):
        far = self.at(2, 0)
        for half in (0, 1):
            self.got(far, half)
            self.put_b(far, half)
        self.across(far)

    def third(self, da):
        down, up = self.at(da, -1), self.at(da, 1)
        self.got(down, 0)
        self.put_b(down, 0, 1)
        self.got(up, 0)
        self.got(up, 1)
        self.put_b(up, 1, -1)
        self.got(down, 1)
        self.across(down)
        self.across(up)

    def fourth(self, da):
        far = self.at(da, 2)
        self.got(far, 0)
        self.got(far, 1)
        self.across(far)

    def stages(self):
        return [
            self.first, lambda: self.third(0), self.second, lambda: self.third(-1), lambda: self.fourth(0),
            lambda: self.third(1), lambda: self.fourth(-1), lambda: self.third(2), lambda: self.fourth(1),
            lambda: self.fourth(2),
        ]

    def last(self):
        for da in range(4):
            for db in range(4):
                self.got(self.sibling(self.at(da, db)), None)

    def drain(self):
        for copy in self.started:
            copy.wait_send()


N_SENDS = 46
N_SEQ = 32


def fused_kernel(q_hbm, kv_hbm, vs_ref, codes_ref, out_ref,
                 k_buf, v_buf, q_ref, parts, plan, slots, bias_v, bias_s, score_v, p_v, p_s, ell, acc, out_buf,
                 local_sem, part_send, part_recv, plan_send, plan_recv, k_send, k_recv, v_send, v_recv, out_send, out_recv):
    me = lax.axis_index("seq")
    z = lax.axis_index("help")
    keys = Gather(me, z, k_buf, ROWS, k_send, k_recv)
    values = Gather(me, z, v_buf, ROWS, v_send, v_recv)
    first_tile = me * TILES_LOCAL
    owner = me // GROUP_HEADS

    barrier = pltpu.get_barrier_semaphore()
    peers = [(keys.at(1, 0), z), (keys.at(-1, 0), z), (keys.at(0, 1), z), (keys.at(0, -1), z), (keys.sibling(me), z)]
    peers += [(me, (z + n) % 8) for n in range(1, 8)]
    for peer in peers:
        pl.semaphore_signal(barrier, inc=1, device_id=peer, device_id_type=MESH)
    for k in range(GROUP_HEADS):
        @pl.when(me != z * GROUP_HEADS + k)
        def _():
            pl.semaphore_signal(barrier, inc=1, device_id=(z * GROUP_HEADS + k, z), device_id_type=MESH)

    k_cols = pl.ds(pl.multiple_of(z * HEAD_DIM, HEAD_DIM), HEAD_DIM)
    v_cols = pl.ds(pl.multiple_of(z * HEAD_DIM + KV_HEADS * HEAD_DIM, HEAD_DIM), HEAD_DIM)
    q_cols = pl.ds(pl.multiple_of(z * GROUP_HEADS * HEAD_DIM, GROUP_HEADS * HEAD_DIM), GROUP_HEADS * HEAD_DIM)
    k_local = pltpu.make_async_copy(kv_hbm.at[:, k_cols], k_buf.at[me, pl.ds(0, ROWS)], local_sem.at[0])
    v_local = pltpu.make_async_copy(kv_hbm.at[:, v_cols], v_buf.at[me], local_sem.at[1])
    q_local = pltpu.make_async_copy(q_hbm.at[:, q_cols], q_ref, local_sem.at[2])
    k_local.start()
    v_local.start()
    q_local.start()

    width = codes_ref.shape[1]
    tile = lax.broadcasted_iota(jnp.int32, (128, width), 0)
    eye = lax.broadcasted_iota(jnp.int32, (128, 128), 0) == lax.broadcasted_iota(jnp.int32, (128, 128), 1)
    named = []
    for n in range(2):
        group = jnp.broadcast_to(codes_ref[...], (128, width)) - (tile + n * 128) * NGROUP
        bits = jnp.where((group >= 0) & (group < NGROUP), lax.shift_left(1, jnp.clip(group, 0, NGROUP - 1)), 0)
        column = jnp.sum(bits, axis=1, keepdims=True)
        named.append(jnp.sum(jnp.where(eye, jnp.broadcast_to(column, (128, 128)), 0), axis=0, keepdims=True))
    parts[z] = jnp.concatenate(named + [jnp.zeros((6, 128), jnp.int32)], axis=0)

    @pl.when(z != owner)
    def _():
        pl.semaphore_wait(barrier, len(peers))

    @pl.when(z == owner)
    def _():
        pl.semaphore_wait(barrier, len(peers) + N_SEQ - 1)

    part = pltpu.make_async_remote_copy(
        src_ref=parts.at[z], dst_ref=parts.at[z], send_sem=part_send, recv_sem=part_recv.at[z],
        device_id=(me, owner), device_id_type=MESH)

    @pl.when(z != owner)
    def _():
        part.start()

    k_local.wait()
    keys.own(0)
    keys.own(1)
    keys.across(me)
    v_local.wait()
    mine = me % GROUP_HEADS

    def plan_copy(k, n):
        return pltpu.make_async_remote_copy(
            src_ref=plan.at[k], dst_ref=plan.at[k], send_sem=plan_send.at[n], recv_sem=plan_recv.at[k],
            device_id=((me + n) % N_SEQ, z), device_id_type=MESH)

    @pl.when(z != owner)
    def _():
        part.wait_send()

    @pl.when(z == owner)
    def _():
        for n in range(1, 8):
            other = (z + n) % 8
            pltpu.make_async_remote_copy(
                src_ref=parts.at[other], dst_ref=parts.at[other], send_sem=part_send, recv_sem=part_recv.at[other],
                device_id=(me, other), device_id_type=MESH).wait_recv()
        total = parts[0]
        for n in range(1, 8):
            total += parts[n]
        plan[mine] = jnp.concatenate([total[:2], vs_ref[...], jnp.zeros((4, 128), jnp.int32)], axis=0)
        for n in range(1, N_SEQ):
            plan_copy(mine, n).start()

    for stage in keys.stages():
        stage()
    values.own(0)
    values.own(1)
    values.across(me)
    keys.last()

    for k in range(GROUP_HEADS):
        @pl.when(me != z * GROUP_HEADS + k)
        def _():
            plan_copy(k, 1).wait_recv()
    slots_copy = pltpu.make_async_copy(plan, slots, local_sem.at[3])
    slots_copy.start()
    make_bias(first_tile, plan, bias_v, bias_s)
    slots_copy.wait()
    q_local.wait()

    stages = values.stages()
    for k in range(GROUP_HEADS):
        score_head(k, first_tile, q_ref, k_buf, slots, bias_v, bias_s, score_v, p_v, p_s, ell)
        for stage in stages[:3]:
            stage()
        stages = stages[3:]
    values.last()

    sent = []
    for k in range(GROUP_HEADS):
        value_head(k, first_tile, v_buf, slots, p_v, p_s, ell, acc, out_buf)
        cols = pl.ds(pl.multiple_of((z * GROUP_HEADS + k) * HEAD_DIM, HEAD_DIM), HEAD_DIM)
        for n in range(1, 8):
            other = (z + n) % 8
            copy = pltpu.make_async_remote_copy(
                src_ref=out_buf.at[k, pl.ds(pl.multiple_of(other * TILE, TILE), TILE)], dst_ref=out_ref.at[:, cols],
                send_sem=out_send.at[k, n], recv_sem=out_recv.at[z, k], device_id=(me, other), device_id_type=MESH)
            copy.start()
            sent.append(copy)
        out_ref[:, cols] = out_buf[k, pl.ds(pl.multiple_of(z * TILE, TILE), TILE), :]
    for k in range(GROUP_HEADS):
        for n in range(1, 8):
            other = (z + n) % 8
            cols = pl.ds(pl.multiple_of((other * GROUP_HEADS + k) * HEAD_DIM, HEAD_DIM), HEAD_DIM)
            pltpu.make_async_remote_copy(
                src_ref=out_buf.at[k, pl.ds(0, TILE)], dst_ref=out_ref.at[:, cols],
                send_sem=out_send.at[k, n], recv_sem=out_recv.at[other, k], device_id=(me, other),
                device_id_type=MESH).wait_recv()
    for copy in sent:
        copy.wait_send()
    keys.drain()
    values.drain()

    @pl.when(z == owner)
    def _():
        for n in range(1, N_SEQ):
            plan_copy(mine, n).wait_send()


def per_device(queries, keys_values, verticals, slashes, units):
    vs = jnp.pad(jnp.concatenate([verticals, slashes]), ((0, 0), (0, 128 - NVERT)))
    vmem = pl.BlockSpec(memory_space=pltpu.VMEM)
    hbm = pl.BlockSpec(memory_space=pl.ANY)
    dma = pltpu.SemaphoreType.DMA
    seq = lax.axis_size("seq")
    return pl.pallas_call(
        fused_kernel,
        out_shape=jax.ShapeDtypeStruct((TILE, HEADS * HEAD_DIM), jnp.bfloat16),
        in_specs=[hbm, hbm, vmem, vmem],
        out_specs=vmem,
        scratch_shapes=[
            pltpu.VMEM((seq, ROWS, HEAD_DIM), jnp.bfloat16),
            pltpu.VMEM((seq, ROWS, HEAD_DIM), jnp.bfloat16),
            pltpu.VMEM((ROWS, GROUP_HEADS * HEAD_DIM), jnp.bfloat16),
            pltpu.VMEM((8, 8, 128), jnp.int32),
            pltpu.VMEM((GROUP_HEADS, 8, 128), jnp.int32),
            pltpu.SMEM((GROUP_HEADS, 8, 128), jnp.int32),
            pltpu.VMEM((GROUP_HEADS, TILES_LOCAL, 1, KEYS), jnp.float32),
            pltpu.VMEM((GROUP_HEADS, TILES_LOCAL, 1, KEYS), jnp.float32),
            pltpu.VMEM((ROWS, KEYS), jnp.float32),
            pltpu.VMEM((GROUP_HEADS, ROWS, KEYS), jnp.bfloat16),
            pltpu.VMEM((GROUP_HEADS, ROWS, KEYS), jnp.bfloat16),
            pltpu.VMEM((GROUP_HEADS, ROWS, HEAD_DIM), jnp.float32),
            pltpu.VMEM((ROWS, HEAD_DIM), jnp.float32),
            pltpu.VMEM((GROUP_HEADS, ROWS, HEAD_DIM), jnp.bfloat16),
            dma((4,)), dma, dma((8,)), dma((N_SEQ,)), dma((GROUP_HEADS,)),
            dma((N_SENDS,)), dma((seq, 2)), dma((N_SENDS,)), dma((seq, 2)),
            dma((GROUP_HEADS, 8)), dma((8, GROUP_HEADS)),
        ],
        compiler_params=pltpu.CompilerParams(
            vmem_limit_bytes=56 * 1024 * 1024, collective_id=0, has_side_effects=True),
        name="fused_attention",
    )(queries, keys_values, vs, units[0])


def solution(mesh):
    in_specs = (
        P("seq", None),
        P("seq", None),
        P("seq", None),
        P("seq", None),
        P("seq", "help", None),
    )
    out_specs = P(("seq", "help"), None)
    return jax.shard_map(
        per_device, mesh=mesh, in_specs=in_specs, out_specs=out_specs, check_vma=False
    )
```

time: 312 us -> 79.7 us (0.26)
  the two profiles are of different devices: /device:TPU:7 before, /device:TPU:1 now
where the time goes in v2:
time: 79.7 us; the launch traced here: 79.6 us
  Pallas kernels  76.5 us (96%)
  local copies, waits for them, and re-layouts  2.44 us (3%)
    pallas_call x1, Pallas kernels, per_device(): pl.pallas_call(fused_kernel, out_shape=jax.ShapeDtypeStruct((TILE, HEADS...  76.5 us
    unnamed x1, local copies, waits for them, and re-layouts  1.87 us

profile of v2, /device:TPU:1, one launch (start us, length us, event | category | flops | bytes accessed | tf_op | source)
XLA Modules:
  0.0 79.6 jit_solution(4101818969949505629)
XLA Ops:
  0.0 0.7 pad_add_fusion
  0.7 0.6 pad.4.vs_ref
  1.2 76.5 %fused_attention.1 = bf16[64,4096]{1,0:T(8,128)(2,1)} custom-call(bf16[512,4096]{1,0:T(8,128)(2,1)} %q_hbm.1, bf16[512,2048]{1,0:T(8,128)(2,1)} %kv_hbm.1, s32[2,128]{1,0:T(2,128)} %pad.4.vs_ref, s32[1,192]{1,0:T(1,128)} %bitcast.1), custom_call_target="tpu_custom_call" | custom-call | tf_op jit(solution)/shard_map/fused_attention/pallas_call | solution.py:386
  77.7 1.9 %copy.7 = bf16[64,4096]{1,0:T(8,128)(2,1)} copy(bf16[64,4096]{1,0:T(8,128)(2,1)} %fused_attention.1) | data formatting | bytes 1048576

commit v3 on v2

--- a/solution.py
+++ b/solution.py
@@ -22,6 +22,7 @@
 ROWS = TILES_LOCAL * TILE
 NEG = -1e30
 HALF = ROWS // 2
+BATCH = TILES_LOCAL // 2
 MESH = pl.DeviceIdType.MESH
 EXP_SCALE = HEAD_DIM ** -0.5 * 1.4426950408889634
 
@@ -68,22 +69,22 @@
     return jnp.concatenate([tile_of(ref, p) for p in places], axis=0)
 
 
-def score_head(k, first_tile, q_ref, k_ref, slots, bias_v, bias_s, score_v, p_v, p_s, ell):
-    q_cols = pl.ds(pl.multiple_of(k * HEAD_DIM, HEAD_DIM), HEAD_DIM)
+def score_vertical(k, q_ref, k_ref, slots, bias_v, score_v):
     for c in range(NCHUNK):
         keys = tiles_of(k_ref, [slots[k, 2, c * CHUNK_TILES + n] for n in range(CHUNK_TILES)])
-        s = dot_t(q_ref[:, q_cols], keys)
+        s = dot_t(q_ref[:, pl.ds(pl.multiple_of(k * HEAD_DIM, HEAD_DIM), HEAD_DIM)], keys)
         cols = slice(c * CHUNK, (c + 1) * CHUNK)
         s = s.reshape(TILES_LOCAL, TILE, CHUNK) + bias_v[k, :, :, cols]
         score_v[:, cols] = s.reshape(ROWS, CHUNK)
+
+
+def score_tiles(k, tiles, first_tile, q_ref, k_ref, slots, bias_s, score_v, p_v, p_s, ell):
     row = lax.broadcasted_iota(jnp.int32, (TILE, CHUNK), 0)
     col = lax.broadcasted_iota(jnp.int32, (TILE, CHUNK), 1)
     diagonal = jnp.where((col < TILE) & (col > row), NEG, 0.0)
-
-    @pl.loop(0, TILES_LOCAL)
-    def _(t):
+    for t in tiles:
         rows = pl.ds(pl.multiple_of(t * TILE, TILE), TILE)
-        q = q_ref[rows, q_cols]
+        q = q_ref[rows, pl.ds(pl.multiple_of(k * HEAD_DIM, HEAD_DIM), HEAD_DIM)]
         parts = []
         for c in range(NCHUNK):
             places = [jnp.maximum(first_tile + t - slots[k, 3, c * CHUNK_TILES + n], 0) for n in range(CHUNK_TILES)]
@@ -110,12 +111,14 @@
     values = tiles_of(v_ref, [slots[k, 2, n] for n in range(NVERT)])
     acc[...] = jnp.dot(p_v[k], values, preferred_element_type=jnp.float32)
 
-    @pl.loop(0, TILES_LOCAL)
-    def _(t):
-        rows = pl.ds(pl.multiple_of(t * TILE, TILE), TILE)
-        places = [jnp.maximum(first_tile + t - slots[k, 3, n], 0) for n in range(NVERT)]
-        o = jnp.dot(p_s[k, rows, :], tiles_of(v_ref, places), preferred_element_type=jnp.float32)
-        out_buf[k, rows, :] = ((o + acc[rows, :]) / ell[k, rows, :]).astype(jnp.bfloat16)
+    @pl.loop(0, TILES_LOCAL // BATCH)
+    def _(batch):
+        for n in range(BATCH):
+            t = batch * BATCH + n
+            rows = pl.ds(pl.multiple_of(t * TILE, TILE), TILE)
+            places = [jnp.maximum(first_tile + t - slots[k, 3, n], 0) for n in range(NVERT)]
+            o = jnp.dot(p_s[k, rows, :], tiles_of(v_ref, places), preferred_element_type=jnp.float32)
+            out_buf[k, rows, :] = ((o + acc[rows, :]) / ell[k, rows, :]).astype(jnp.bfloat16)
 
 
 class Gather:
@@ -155,7 +158,7 @@
     def put(self, shard, half, target):
         copy = self.copy(shard, half, target, len(self.started))
         copy.start()
-        self.started.append(copy)
+        self.started.append(half)
 
     def got(self, shard, half):
         self.copy(shard, half, self.sibling(self.me), 0).wait_recv()
@@ -226,15 +229,15 @@
                 self.got(self.sibling(self.at(da, db)), None)
 
     def drain(self):
-        for copy in self.started:
-            copy.wait_send()
+        for n, half in enumerate(self.started):
+            self.copy(self.me, half, self.sibling(self.me), n).wait_send()
 
 
 N_SENDS = 46
 N_SEQ = 32
 
 
-def fused_kernel(q_hbm, kv_hbm, vs_ref, codes_ref, out_ref,
+def fused_kernel(q_hbm, kv_hbm, verts_ref, slashes_ref, codes_ref, out_ref,
                  k_buf, v_buf, q_ref, parts, plan, slots, bias_v, bias_s, score_v, p_v, p_s, ell, acc, out_buf,
                  local_sem, part_send, part_recv, plan_send, plan_recv, k_send, k_recv, v_send, v_recv, out_send, out_recv):
     me = lax.axis_index("seq")
@@ -295,7 +298,6 @@
     keys.own(0)
     keys.own(1)
     keys.across(me)
-    v_local.wait()
     mine = me % GROUP_HEADS
 
     def plan_copy(k, n):
@@ -317,48 +319,70 @@
         total = parts[0]
         for n in range(1, 8):
             total += parts[n]
-        plan[mine] = jnp.concatenate([total[:2], vs_ref[...], jnp.zeros((4, 128), jnp.int32)], axis=0)
+        plan[mine] = total
+        plan[mine, 2:3, 0:NVERT] = verts_ref[...]
+        plan[mine, 3:4, 0:NVERT] = slashes_ref[...]
         for n in range(1, N_SEQ):
             plan_copy(mine, n).start()
 
-    for stage in keys.stages():
+    stages = keys.stages()
+    for stage in stages[:4]:
         stage()
-    values.own(0)
-    values.own(1)
-    values.across(me)
-    keys.last()
-
     for k in range(GROUP_HEADS):
         @pl.when(me != z * GROUP_HEADS + k)
         def _():
             plan_copy(k, 1).wait_recv()
     slots_copy = pltpu.make_async_copy(plan, slots, local_sem.at[3])
     slots_copy.start()
+    for stage in stages[4:8]:
+        stage()
+    v_local.wait()
+    values.own(0)
+    values.own(1)
+    values.across(me)
     make_bias(first_tile, plan, bias_v, bias_s)
+    for stage in stages[8:]:
+        stage()
     slots_copy.wait()
     q_local.wait()
+    keys.last()
 
     stages = values.stages()
-    for k in range(GROUP_HEADS):
-        score_head(k, first_tile, q_ref, k_buf, slots, bias_v, bias_s, score_v, p_v, p_s, ell)
-        for stage in stages[:3]:
-            stage()
-        stages = stages[3:]
+    gaps = [stages[:1], stages[1:3], stages[3:4], stages[4:6], stages[6:8], stages[8:9], stages[9:], []]
+
+    @pl.loop(0, GROUP_HEADS)
+    def _(k):
+        score_vertical(k, q_ref, k_buf, slots, bias_v, score_v)
+
+        @pl.loop(0, TILES_LOCAL // BATCH)
+        def _(batch):
+            tiles = [batch * BATCH + n for n in range(BATCH)]
+            score_tiles(k, tiles, first_tile, q_ref, k_buf, slots, bias_s, score_v, p_v, p_s, ell)
+            for n, gap in enumerate(gaps):
+                @pl.when(k * (TILES_LOCAL // BATCH) + batch == n)
+                def _():
+                    for stage in gap:
+                        stage()
+
     values.last()
 
-    sent = []
-    for k in range(GROUP_HEADS):
+    def out_copy(k, n):
+        other = (z + n) % 8
+        return pltpu.make_async_remote_copy(
+            src_ref=out_buf.at[k, pl.ds(pl.multiple_of(other * TILE, TILE), TILE)],
+            dst_ref=out_ref.at[:, pl.ds(pl.multiple_of((z * GROUP_HEADS + k) * HEAD_DIM, HEAD_DIM), HEAD_DIM)],
+            send_sem=out_send.at[k, n], recv_sem=out_recv.at[z, k], device_id=(me, other), device_id_type=MESH)
+
+    @pl.loop(0, GROUP_HEADS)
+    def _(k):
         value_head(k, first_tile, v_buf, slots, p_v, p_s, ell, acc, out_buf)
+        for n in range(1, 8):
+            out_copy(k, n).start()
         cols = pl.ds(pl.multiple_of((z * GROUP_HEADS + k) * HEAD_DIM, HEAD_DIM), HEAD_DIM)
-        for n in range(1, 8):
-            other = (z + n) % 8
-            copy = pltpu.make_async_remote_copy(
-                src_ref=out_buf.at[k, pl.ds(pl.multiple_of(other * TILE, TILE), TILE)], dst_ref=out_ref.at[:, cols],
-                send_sem=out_send.at[k, n], recv_sem=out_recv.at[z, k], device_id=(me, other), device_id_type=MESH)
-            copy.start()
-            sent.append(copy)
         out_ref[:, cols] = out_buf[k, pl.ds(pl.multiple_of(z * TILE, TILE), TILE), :]
-    for k in range(GROUP_HEADS):
+
+    @pl.loop(0, GROUP_HEADS)
+    def _(k):
         for n in range(1, 8):
             other = (z + n) % 8
             cols = pl.ds(pl.multiple_of((other * GROUP_HEADS + k) * HEAD_DIM, HEAD_DIM), HEAD_DIM)
@@ -366,8 +390,8 @@
                 src_ref=out_buf.at[k, pl.ds(0, TILE)], dst_ref=out_ref.at[:, cols],
                 send_sem=out_send.at[k, n], recv_sem=out_recv.at[other, k], device_id=(me, other),
                 device_id_type=MESH).wait_recv()
-    for copy in sent:
-        copy.wait_send()
+            out_copy(k, n).wait_send()
+
     keys.drain()
     values.drain()
 
@@ -378,7 +402,6 @@
 
 
 def per_device(queries, keys_values, verticals, slashes, units):
-    vs = jnp.pad(jnp.concatenate([verticals, slashes]), ((0, 0), (0, 128 - NVERT)))
     vmem = pl.BlockSpec(memory_space=pltpu.VMEM)
     hbm = pl.BlockSpec(memory_space=pl.ANY)
     dma = pltpu.SemaphoreType.DMA
@@ -386,7 +409,7 @@
     return pl.pallas_call(
         fused_kernel,
         out_shape=jax.ShapeDtypeStruct((TILE, HEADS * HEAD_DIM), jnp.bfloat16),
-        in_specs=[hbm, hbm, vmem, vmem],
+        in_specs=[hbm, hbm, vmem, vmem, vmem],
         out_specs=vmem,
         scratch_shapes=[
             pltpu.VMEM((seq, ROWS, HEAD_DIM), jnp.bfloat16),
@@ -410,7 +433,7 @@
         compiler_params=pltpu.CompilerParams(
             vmem_limit_bytes=56 * 1024 * 1024, collective_id=0, has_side_effects=True),
         name="fused_attention",
-    )(queries, keys_values, vs, units[0])
+    )(queries, keys_values, verticals, slashes, units[0])
 
 
 def solution(mesh):

time: 79.7 us -> 67.9 us (0.85)
  Pallas kernels: 76.5 us -> 65.9 us
    pallas_call x1, Pallas kernels: 76.5 us -> 65.9 us  [per_device(): pl.pallas_call(fused_kernel, out_shape=jax.ShapeDtypeStruct((TILE, HEADS...]
where the time goes in v3:
time: 67.9 us; the launch traced here: 67.7 us
  Pallas kernels  65.9 us (97%)
  local copies, waits for them, and re-layouts  1.87 us (3%)
    pallas_call x1, Pallas kernels, per_device(): pl.pallas_call(fused_kernel, out_shape=jax.ShapeDtypeStruct((TILE, HEADS...  65.9 us
    unnamed x1, local copies, waits for them, and re-layouts  1.87 us

profile of v3, /device:TPU:1, one launch (start us, length us, event | category | flops | bytes accessed | tf_op | source)
XLA Modules:
  0.0 67.7 jit_solution(10697193250309721291)
XLA Ops:
  0.0 65.9 %fused_attention.1 = bf16[64,4096]{1,0:T(8,128)(2,1)} custom-call(bf16[512,4096]{1,0:T(8,128)(2,1)} %q_hbm.1, bf16[512,2048]{1,0:T(8,128)(2,1)} %kv_hbm.1, s32[1,24]{1,0:T(1,128)} %verts_ref.1, s32[1,24]{1,0:T(1,128)} %slashes_ref.1, s32[1,192]{1,0:T(1,128)} %bitcast.1), custom_call_target="tpu_custom_call" | custom-call | tf_op jit(solution)/shard_map/fused_attention/pallas_call | solution.py:409
  65.9 1.9 %copy.7 = bf16[64,4096]{1,0:T(8,128)(2,1)} copy(bf16[64,4096]{1,0:T(8,128)(2,1)} %fused_attention.1) | data formatting | bytes 1048576

commit v4 on v3

--- a/solution.py
+++ b/solution.py
@@ -163,65 +163,68 @@
     def got(self, shard, half):
         self.copy(shard, half, self.sibling(self.me), 0).wait_recv()
 
-    def put_a(self, shard, half, da):
-        self.put(shard, half, self.at(da, 0))
-
-    def put_b(self, shard, half, way=None):
-        for db in (1, -1) if way is None else (way,):
+    def put_a(self, shard, half, ways):
+        for da in ways:
+            self.put(shard, half, self.at(da, 0))
+
+    def put_b(self, shard, half, ways):
+        for db in ways:
             self.put(shard, half, self.at(0, db))
 
     def across(self, shard):
         self.put(shard, None, self.sibling(self.me))
 
-    def own(self, half):
-        mine = self.me
-        self.put_a(mine, half, 1)
-        self.put_a(mine, half, -1)
-        self.put_b(mine, half)
-
-    def first(self):
-        left, right = self.at(-1, 0), self.at(1, 0)
-        self.got(left, 0)
-        self.put_a(left, 0, 1)
-        self.got(right, 0)
-        self.got(right, 1)
-        self.put_a(right, 1, -1)
-        self.got(left, 1)
-        for shard in (left, right):
+    def own(self):
+        for half in (0, 1):
+            self.put_a(self.me, half, (1, -1))
+            self.put_b(self.me, half, (1, -1))
+        for half in (0, 1):
+            self.put_a(self.me, half, (2,))
+        self.across(self.me)
+
+    def near(self, da):
+        shard = self.at(da, 0)
+        for half in (0, 1):
+            self.got(shard, half)
+            self.put_b(shard, half, (1, -1))
+        if da == 2:
             for half in (0, 1):
-                self.put_b(shard, half)
-            self.across(shard)
-
-    def second(self):
-        far = self.at(2, 0)
-        for half in (0, 1):
-            self.got(far, half)
-            self.put_b(far, half)
-        self.across(far)
-
-    def third(self, da):
+                self.put_b(shard, half, (2,))
+        self.across(shard)
+
+    def pass_on(self, da):
         down, up = self.at(da, -1), self.at(da, 1)
         self.got(down, 0)
-        self.put_b(down, 0, 1)
+        if da != 2:
+            self.put_b(down, 0, (1,))
         self.got(up, 0)
         self.got(up, 1)
-        self.put_b(up, 1, -1)
+        if da != 2:
+            self.put_b(up, 1, (-1,))
         self.got(down, 1)
         self.across(down)
         self.across(up)
 
-    def fourth(self, da):
-        far = self.at(da, 2)
-        self.got(far, 0)
-        self.got(far, 1)
-        self.across(far)
-
-    def stages(self):
-        return [
-            self.first, lambda: self.third(0), self.second, lambda: self.third(-1), lambda: self.fourth(0),
-            lambda: self.third(1), lambda: self.fourth(-1), lambda: self.third(2), lambda: self.fourth(1),
-            lambda: self.fourth(2),
-        ]
+    def far(self, da):
+        shard = self.at(da, 2)
+        self.got(shard, 0)
+        self.got(shard, 1)
+        self.across(shard)
+
+    def sends(self):
+        self.near(-1)
+        self.near(1)
+        self.pass_on(0)
+        self.near(2)
+        self.pass_on(-1)
+        self.pass_on(1)
+
+    def ends(self):
+        self.far(0)
+        self.pass_on(2)
+        self.far(-1)
+        self.far(1)
+        self.far(2)
 
     def last(self):
         for da in range(4):
@@ -233,7 +236,7 @@
             self.copy(self.me, half, self.sibling(self.me), n).wait_send()
 
 
-N_SENDS = 46
+N_SENDS = 49
 N_SEQ = 32
 
 
@@ -248,7 +251,7 @@
     owner = me // GROUP_HEADS
 
     barrier = pltpu.get_barrier_semaphore()
-    peers = [(keys.at(1, 0), z), (keys.at(-1, 0), z), (keys.at(0, 1), z), (keys.at(0, -1), z), (keys.sibling(me), z)]
+    peers = [(keys.at(n, 0), z) for n in (1, 2, 3)] + [(keys.at(0, n), z) for n in (1, 2, 3)] + [(keys.sibling(me), z)]
     peers += [(me, (z + n) % 8) for n in range(1, 8)]
     for peer in peers:
         pl.semaphore_signal(barrier, inc=1, device_id=peer, device_id_type=MESH)
@@ -295,9 +298,7 @@
         part.start()
 
     k_local.wait()
-    keys.own(0)
-    keys.own(1)
-    keys.across(me)
+    keys.own()
     mine = me % GROUP_HEADS
 
     def plan_copy(k, n):
@@ -325,46 +326,36 @@
         for n in range(1, N_SEQ):
             plan_copy(mine, n).start()
 
-    stages = keys.stages()
-    for stage in stages[:4]:
-        stage()
+    keys.sends()
+    v_local.wait()
+    values.own()
     for k in range(GROUP_HEADS):
         @pl.when(me != z * GROUP_HEADS + k)
         def _():
             plan_copy(k, 1).wait_recv()
     slots_copy = pltpu.make_async_copy(plan, slots, local_sem.at[3])
     slots_copy.start()
-    for stage in stages[4:8]:
-        stage()
-    v_local.wait()
-    values.own(0)
-    values.own(1)
-    values.across(me)
     make_bias(first_tile, plan, bias_v, bias_s)
-    for stage in stages[8:]:
-        stage()
+    keys.ends()
     slots_copy.wait()
     q_local.wait()
     keys.last()
 
-    stages = values.stages()
-    gaps = [stages[:1], stages[1:3], stages[3:4], stages[4:6], stages[6:8], stages[8:9], stages[9:], []]
-
-    @pl.loop(0, GROUP_HEADS)
-    def _(k):
-        score_vertical(k, q_ref, k_buf, slots, bias_v, score_v)
-
-        @pl.loop(0, TILES_LOCAL // BATCH)
-        def _(batch):
-            tiles = [batch * BATCH + n for n in range(BATCH)]
-            score_tiles(k, tiles, first_tile, q_ref, k_buf, slots, bias_s, score_v, p_v, p_s, ell)
-            for n, gap in enumerate(gaps):
-                @pl.when(k * (TILES_LOCAL // BATCH) + batch == n)
-                def _():
-                    for stage in gap:
-                        stage()
-
-    values.last()
+    def gap(n):
+        if n == 0:
+            values.near(-1)
+            values.near(1)
+        elif n == 1:
+            values.pass_on(0)
+            values.near(2)
+        elif n == 3:
+            values.pass_on(-1)
+            values.pass_on(1)
+        elif n == 4:
+            keys.drain()
+        elif n == 5:
+            values.ends()
+            values.last()
 
     def out_copy(k, n):
         other = (z + n) % 8
@@ -373,13 +364,37 @@
             dst_ref=out_ref.at[:, pl.ds(pl.multiple_of((z * GROUP_HEADS + k) * HEAD_DIM, HEAD_DIM), HEAD_DIM)],
             send_sem=out_send.at[k, n], recv_sem=out_recv.at[z, k], device_id=(me, other), device_id_type=MESH)
 
-    @pl.loop(0, GROUP_HEADS)
-    def _(k):
-        value_head(k, first_tile, v_buf, slots, p_v, p_s, ell, acc, out_buf)
-        for n in range(1, 8):
-            out_copy(k, n).start()
-        cols = pl.ds(pl.multiple_of((z * GROUP_HEADS + k) * HEAD_DIM, HEAD_DIM), HEAD_DIM)
-        out_ref[:, cols] = out_buf[k, pl.ds(pl.multiple_of(z * TILE, TILE), TILE), :]
+    @pl.loop(0, 2 * GROUP_HEADS)
+    def _(step):
+        @pl.when((step < 3) | (step == 6))
+        def _():
+            k = step - 3 * (step // 6)
+            score_vertical(k, q_ref, k_buf, slots, bias_v, score_v)
+
+            @pl.loop(0, TILES_LOCAL // BATCH)
+            def _(batch):
+                tiles = [batch * BATCH + n for n in range(BATCH)]
+                score_tiles(k, tiles, first_tile, q_ref, k_buf, slots, bias_s, score_v, p_v, p_s, ell)
+                for n in (0, 1, 3, 4, 5):
+                    @pl.when(k * (TILES_LOCAL // BATCH) + batch == n)
+                    def _():
+                        gap(n)
+
+        @pl.when(((step > 2) & (step < 6)) | (step == 7))
+        def _():
+            k = step - 3 - step // 7
+            value_head(k, first_tile, v_buf, slots, p_v, p_s, ell, acc, out_buf)
+            for n in range(1, 8):
+                out_copy(k, n).start()
+            cols = pl.ds(pl.multiple_of((z * GROUP_HEADS + k) * HEAD_DIM, HEAD_DIM), HEAD_DIM)
+            out_ref[:, cols] = out_buf[k, pl.ds(pl.multiple_of(z * TILE, TILE), TILE), :]
+
+    values.drain()
+
+    @pl.when(z == owner)
+    def _():
+        for n in range(1, N_SEQ):
+            plan_copy(mine, n).wait_send()
 
     @pl.loop(0, GROUP_HEADS)
     def _(k):
@@ -391,14 +406,6 @@
                 send_sem=out_send.at[k, n], recv_sem=out_recv.at[other, k], device_id=(me, other),
                 device_id_type=MESH).wait_recv()
             out_copy(k, n).wait_send()
-
-    keys.drain()
-    values.drain()
-
-    @pl.when(z == owner)
-    def _():
-        for n in range(1, N_SEQ):
-            plan_copy(mine, n).wait_send()
 
 
 def per_device(queries, keys_values, verticals, slashes, units):

time: 67.9 us -> 65.5 us (0.965)
  Pallas kernels: 65.9 us -> 63.5 us
    pallas_call x1, Pallas kernels: 65.9 us -> 63.5 us  [per_device(): pl.pallas_call(fused_kernel, out_shape=jax.ShapeDtypeStruct((TILE, HEADS...]
where the time goes in v4:
time: 65.5 us; the launch traced here: 65.3 us
  Pallas kernels  63.5 us (97%)
  local copies, waits for them, and re-layouts  1.87 us (3%)
    pallas_call x1, Pallas kernels, per_device(): pl.pallas_call(fused_kernel, out_shape=jax.ShapeDtypeStruct((TILE, HEADS...  63.5 us
    unnamed x1, local copies, waits for them, and re-layouts  1.87 us

profile of v4, /device:TPU:1, one launch (start us, length us, event | category | flops | bytes accessed | tf_op | source)
XLA Modules:
  0.0 65.3 jit_solution(1336956977771688239)
XLA Ops:
  0.0 63.5 %fused_attention.1 = bf16[64,4096]{1,0:T(8,128)(2,1)} custom-call(bf16[512,4096]{1,0:T(8,128)(2,1)} %q_hbm.1, bf16[512,2048]{1,0:T(8,128)(2,1)} %kv_hbm.1, s32[1,24]{1,0:T(1,128)} %verts_ref.1, s32[1,24]{1,0:T(1,128)} %slashes_ref.1, s32[1,192]{1,0:T(1,128)} %bitcast.1), custom_call_target="tpu_custom_call" | custom-call | tf_op jit(solution)/shard_map/fused_attention/pallas_call | solution.py:416
  63.5 1.9 %copy.7 = bf16[64,4096]{1,0:T(8,128)(2,1)} copy(bf16[64,4096]{1,0:T(8,128)(2,1)} %fused_attention.1) | data formatting | bytes 1048576

commit v5 on v4

--- a/solution.py
+++ b/solution.py
@@ -69,9 +69,10 @@
     return jnp.concatenate([tile_of(ref, p) for p in places], axis=0)
 
 
-def score_vertical(k, q_ref, k_ref, slots, bias_v, score_v):
+def score_vertical(k, first_tile, q_ref, k_ref, slots, bias_v, score_v):
     for c in range(NCHUNK):
-        keys = tiles_of(k_ref, [slots[k, 2, c * CHUNK_TILES + n] for n in range(CHUNK_TILES)])
+        places = [slots[k, 2, c * CHUNK_TILES + n] for n in range(CHUNK_TILES)]
+        keys = tiles_of(k_ref, [jnp.minimum(p, first_tile + TILES_LOCAL - 1) for p in places])
         s = dot_t(q_ref[:, pl.ds(pl.multiple_of(k * HEAD_DIM, HEAD_DIM), HEAD_DIM)], keys)
         cols = slice(c * CHUNK, (c + 1) * CHUNK)
         s = s.reshape(TILES_LOCAL, TILE, CHUNK) + bias_v[k, :, :, cols]
@@ -107,18 +108,25 @@
         ell[k, rows, :] = jnp.broadcast_to(jnp.sum(total, axis=1, keepdims=True), (TILE, HEAD_DIM))
 
 
-def value_head(k, first_tile, v_ref, slots, p_v, p_s, ell, acc, out_buf):
-    values = tiles_of(v_ref, [slots[k, 2, n] for n in range(NVERT)])
+def value_head(k, first_tile, z, v_ref, slots, p_v, p_s, ell, acc, out_buf, send):
+    places = [slots[k, 2, n] for n in range(NVERT)]
+    values = tiles_of(v_ref, [jnp.minimum(p, first_tile + TILES_LOCAL - 1) for p in places])
     acc[...] = jnp.dot(p_v[k], values, preferred_element_type=jnp.float32)
 
     @pl.loop(0, TILES_LOCAL // BATCH)
     def _(batch):
-        for n in range(BATCH):
-            t = batch * BATCH + n
+        for m in range(BATCH):
+            t = (z + 1 + batch * BATCH + m) % TILES_LOCAL
             rows = pl.ds(pl.multiple_of(t * TILE, TILE), TILE)
             places = [jnp.maximum(first_tile + t - slots[k, 3, n], 0) for n in range(NVERT)]
             o = jnp.dot(p_s[k, rows, :], tiles_of(v_ref, places), preferred_element_type=jnp.float32)
             out_buf[k, rows, :] = ((o + acc[rows, :]) / ell[k, rows, :]).astype(jnp.bfloat16)
+        for m in range(BATCH):
+            step = batch * BATCH + m + 1
+
+            @pl.when(step < TILES_LOCAL)
+            def _():
+                send(k, step)
 
 
 class Gather:
@@ -155,65 +163,94 @@
             recv_sem=self.recv.at[shard, 0 if half is None else half],
             device_id=(target, self.z), device_id_type=MESH)
 
-    def put(self, shard, half, target):
-        copy = self.copy(shard, half, target, len(self.started))
-        copy.start()
-        self.started.append(half)
-
-    def got(self, shard, half):
-        self.copy(shard, half, self.sibling(self.me), 0).wait_recv()
-
-    def put_a(self, shard, half, ways):
-        for da in ways:
-            self.put(shard, half, self.at(da, 0))
-
-    def put_b(self, shard, half, ways):
-        for db in ways:
-            self.put(shard, half, self.at(0, db))
-
-    def across(self, shard):
-        self.put(shard, None, self.sibling(self.me))
+    def need(self, device, shard):
+        return shard // 2 <= device // 2
+
+    def put(self, shard, half, target, cond):
+        n = len(self.started)
+
+        @pl.when(cond())
+        def _():
+            self.copy(shard, half, target, n).start()
+
+        self.started.append((half, cond))
+
+    def got(self, shard, half, cond):
+        @pl.when(cond())
+        def _():
+            self.copy(shard, half, self.sibling(self.me), 0).wait_recv()
+
+    def last_of_ring(self, da):
+        return self.at(da, 3 - self.b)
+
+    def passes(self, da, db, half):
+        return da != 2 and (half, db) in ((0, 1), (1, -1))
+
+    def put_a(self, half, da):
+        self.put(self.me, half, self.at(da, 0), lambda: self.need(self.last_of_ring(da), self.me))
+
+    def put_b(self, da, half, db):
+        def cond():
+            shard = self.at(da, 0)
+            if self.passes(da, db, half):
+                return self.need(self.at(0, db), shard) | self.need(self.at(0, 2), shard)
+            return self.need(self.at(0, db), shard)
+
+        self.put(self.at(da, 0), half, self.at(0, db), cond)
+
+    def across(self, da, db):
+        self.put(self.at(da, db), None, self.sibling(self.me), lambda: self.need(self.me, self.at(da, db)))
 
     def own(self):
         for half in (0, 1):
-            self.put_a(self.me, half, (1, -1))
-            self.put_b(self.me, half, (1, -1))
+            for way in (1, -1):
+                self.put_a(half, way)
+            for way in (1, -1):
+                self.put_b(0, half, way)
         for half in (0, 1):
-            self.put_a(self.me, half, (2,))
-        self.across(self.me)
-
-    def near(self, da):
-        shard = self.at(da, 0)
+            self.put_a(half, 2)
+        self.across(0, 0)
+
+    def near(self, *das):
         for half in (0, 1):
-            self.got(shard, half)
-            self.put_b(shard, half, (1, -1))
-        if da == 2:
-            for half in (0, 1):
-                self.put_b(shard, half, (2,))
-        self.across(shard)
+            for da in das:
+                self.got(self.at(da, 0), half, lambda: self.need(self.last_of_ring(0), self.at(da, 0)))
+                for way in (1, -1):
+                    self.put_b(da, half, way)
+        for da in das:
+            if da == 2:
+                for half in (0, 1):
+                    self.put_b(da, half, 2)
+            self.across(da, 0)
+
+    def from_b(self, da, db, half):
+        shard, beyond = self.at(da, db), self.at(0, -db)
+        passes = self.passes(da, -db, half)
+
+        def cond():
+            if passes:
+                return self.need(self.me, shard) | self.need(beyond, shard)
+            return self.need(self.me, shard)
+
+        self.got(shard, half, cond)
+        if passes:
+            self.put(shard, half, beyond, lambda: self.need(self.at(0, -db), self.at(da, db)))
 
     def pass_on(self, da):
-        down, up = self.at(da, -1), self.at(da, 1)
-        self.got(down, 0)
-        if da != 2:
-            self.put_b(down, 0, (1,))
-        self.got(up, 0)
-        self.got(up, 1)
-        if da != 2:
-            self.put_b(up, 1, (-1,))
-        self.got(down, 1)
-        self.across(down)
-        self.across(up)
+        self.from_b(da, -1, 0)
+        self.from_b(da, 1, 0)
+        self.from_b(da, 1, 1)
+        self.from_b(da, -1, 1)
+        self.across(da, -1)
+        self.across(da, 1)
 
     def far(self, da):
-        shard = self.at(da, 2)
-        self.got(shard, 0)
-        self.got(shard, 1)
-        self.across(shard)
+        for half in (0, 1):
+            self.got(self.at(da, 2), half, lambda: self.need(self.me, self.at(da, 2)))
+        self.across(da, 2)
 
     def sends(self):
-        self.near(-1)
-        self.near(1)
+        self.near(-1, 1)
         self.pass_on(0)
         self.near(2)
         self.pass_on(-1)
@@ -229,11 +266,14 @@
     def last(self):
         for da in range(4):
             for db in range(4):
-                self.got(self.sibling(self.at(da, db)), None)
+                shard = self.sibling(self.at(da, db))
+                self.got(shard, None, lambda: self.need(self.me, shard))
 
     def drain(self):
-        for n, half in enumerate(self.started):
-            self.copy(self.me, half, self.sibling(self.me), n).wait_send()
+        for n, (half, cond) in enumerate(self.started):
+            @pl.when(cond())
+            def _():
+                self.copy(self.me, half, self.sibling(self.me), n).wait_send()
 
 
 N_SENDS = 49
@@ -343,8 +383,7 @@
 
     def gap(n):
         if n == 0:
-            values.near(-1)
-            values.near(1)
+            values.near(-1, 1)
         elif n == 1:
             values.pass_on(0)
             values.near(2)
@@ -369,7 +408,7 @@
         @pl.when((step < 3) | (step == 6))
         def _():
             k = step - 3 * (step // 6)
-            score_vertical(k, q_ref, k_buf, slots, bias_v, score_v)
+            score_vertical(k, first_tile, q_ref, k_buf, slots, bias_v, score_v)
 
             @pl.loop(0, TILES_LOCAL // BATCH)
             def _(batch):
@@ -383,9 +422,7 @@
         @pl.when(((step > 2) & (step < 6)) | (step == 7))
         def _():
             k = step - 3 - step // 7
-            value_head(k, first_tile, v_buf, slots, p_v, p_s, ell, acc, out_buf)
-            for n in range(1, 8):
-                out_copy(k, n).start()
+            value_head(k, first_tile, z, v_buf, slots, p_v, p_s, ell, acc, out_buf, lambda k, n: out_copy(k, n).start())
             cols = pl.ds(pl.multiple_of((z * GROUP_HEADS + k) * HEAD_DIM, HEAD_DIM), HEAD_DIM)
             out_ref[:, cols] = out_buf[k, pl.ds(pl.multiple_of(z * TILE, TILE), TILE), :]
 

time: 65.5 us -> 61.5 us (0.939)
  the two profiles are of different devices: /device:TPU:1 before, /device:TPU:7 now
where the time goes in v5:
time: 61.5 us; the launch traced here: 61.4 us
  Pallas kernels  59.5 us (97%)
  local copies, waits for them, and re-layouts  1.87 us (3%)
    pallas_call x1, Pallas kernels, per_device(): pl.pallas_call(fused_kernel, out_shape=jax.ShapeDtypeStruct((TILE, HEADS...  59.5 us
    unnamed x1, local copies, waits for them, and re-layouts  1.87 us

profile of v5, /device:TPU:7, one launch (start us, length us, event | category | flops | bytes accessed | tf_op | source)
XLA Modules:
  0.0 61.4 jit_solution(9569560456132416175)
XLA Ops:
  0.0 59.5 %fused_attention.1 = bf16[64,4096]{1,0:T(8,128)(2,1)} custom-call(bf16[512,4096]{1,0:T(8,128)(2,1)} %q_hbm.1, bf16[512,2048]{1,0:T(8,128)(2,1)} %kv_hbm.1, s32[1,24]{1,0:T(1,128)} %verts_ref.1, s32[1,24]{1,0:T(1,128)} %slashes_ref.1, s32[1,192]{1,0:T(1,128)} %bitcast.1), custom_call_target="tpu_custom_call" | custom-call | tf_op jit(solution)/shard_map/fused_attention/pallas_call | solution.py:453
  59.5 1.9 %copy.7 = bf16[64,4096]{1,0:T(8,128)(2,1)} copy(bf16[64,4096]{1,0:T(8,128)(2,1)} %fused_attention.1) | data formatting | bytes 1048576

commit v6 on v5

--- a/solution.py
+++ b/solution.py
@@ -379,18 +379,17 @@
     keys.ends()
     slots_copy.wait()
     q_local.wait()
+    values.near(-1, 1)
     keys.last()
 
     def gap(n):
         if n == 0:
-            values.near(-1, 1)
-        elif n == 1:
             values.pass_on(0)
             values.near(2)
-        elif n == 3:
+        elif n == 2:
             values.pass_on(-1)
             values.pass_on(1)
-        elif n == 4:
+        elif n == 3:
             keys.drain()
         elif n == 5:
             values.ends()
@@ -414,7 +413,7 @@
             def _(batch):
                 tiles = [batch * BATCH + n for n in range(BATCH)]
                 score_tiles(k, tiles, first_tile, q_ref, k_buf, slots, bias_s, score_v, p_v, p_s, ell)
-                for n in (0, 1, 3, 4, 5):
+                for n in (0, 2, 3, 5):
                     @pl.when(k * (TILES_LOCAL // BATCH) + batch == n)
                     def _():
                         gap(n)

time: 61.5 us -> 60.1 us (0.977)
  Pallas kernels: 59.5 us -> 58.1 us
    pallas_call x1, Pallas kernels: 59.5 us -> 58.1 us  [per_device(): pl.pallas_call(fused_kernel, out_shape=jax.ShapeDtypeStruct((TILE, HEADS...]
where the time goes in v6:
time: 60.1 us; the launch traced here: 60 us
  Pallas kernels  58.1 us (97%)
  local copies, waits for them, and re-layouts  1.87 us (3%)
    pallas_call x1, Pallas kernels, per_device(): pl.pallas_call(fused_kernel, out_shape=jax.ShapeDtypeStruct((TILE, HEADS...  58.1 us
    unnamed x1, local copies, waits for them, and re-layouts  1.87 us

profile of v6, /device:TPU:7, one launch (start us, length us, event | category | flops | bytes accessed | tf_op | source)
XLA Modules:
  0.0 60.0 jit_solution(8582269329913392484)
XLA Ops:
  0.0 58.1 %fused_attention.1 = bf16[64,4096]{1,0:T(8,128)(2,1)} custom-call(bf16[512,4096]{1,0:T(8,128)(2,1)} %q_hbm.1, bf16[512,2048]{1,0:T(8,128)(2,1)} %kv_hbm.1, s32[1,24]{1,0:T(1,128)} %verts_ref.1, s32[1,24]{1,0:T(1,128)} %slashes_ref.1, s32[1,192]{1,0:T(1,128)} %bitcast.1), custom_call_target="tpu_custom_call" | custom-call | tf_op jit(solution)/shard_map/fused_attention/pallas_call | solution.py:452
  58.1 1.9 %copy.7 = bf16[64,4096]{1,0:T(8,128)(2,1)} copy(bf16[64,4096]{1,0:T(8,128)(2,1)} %fused_attention.1) | data formatting | bytes 1048576

commit v7 on v6

--- a/solution.py
+++ b/solution.py
@@ -111,22 +111,24 @@
 def value_head(k, first_tile, z, v_ref, slots, p_v, p_s, ell, acc, out_buf, send):
     places = [slots[k, 2, n] for n in range(NVERT)]
     values = tiles_of(v_ref, [jnp.minimum(p, first_tile + TILES_LOCAL - 1) for p in places])
-    acc[...] = jnp.dot(p_v[k], values, preferred_element_type=jnp.float32)
 
     @pl.loop(0, TILES_LOCAL // BATCH)
     def _(batch):
+        first = (z // BATCH + 1 + batch) % (TILES_LOCAL // BATCH) * BATCH
+        half = pl.ds(pl.multiple_of(first * TILE, BATCH * TILE), BATCH * TILE)
+        acc[half, :] = jnp.dot(p_v[k, half, :], values, preferred_element_type=jnp.float32)
         for m in range(BATCH):
-            t = (z + 1 + batch * BATCH + m) % TILES_LOCAL
+            t = first + m
             rows = pl.ds(pl.multiple_of(t * TILE, TILE), TILE)
             places = [jnp.maximum(first_tile + t - slots[k, 3, n], 0) for n in range(NVERT)]
             o = jnp.dot(p_s[k, rows, :], tiles_of(v_ref, places), preferred_element_type=jnp.float32)
             out_buf[k, rows, :] = ((o + acc[rows, :]) / ell[k, rows, :]).astype(jnp.bfloat16)
         for m in range(BATCH):
-            step = batch * BATCH + m + 1
-
-            @pl.when(step < TILES_LOCAL)
+            t = first + m
+
+            @pl.when(t != z)
             def _():
-                send(k, step)
+                send(k, (t - z + TILES_LOCAL) % TILES_LOCAL)
 
 
 class Gather:
@@ -215,12 +217,9 @@
         for half in (0, 1):
             for da in das:
                 self.got(self.at(da, 0), half, lambda: self.need(self.last_of_ring(0), self.at(da, 0)))
-                for way in (1, -1):
+                for way in (2, 1, -1) if da == 2 else (1, -1):
                     self.put_b(da, half, way)
         for da in das:
-            if da == 2:
-                for half in (0, 1):
-                    self.put_b(da, half, 2)
             self.across(da, 0)
 
     def from_b(self, da, db, half):

time: 60.1 us -> 58.4 us (0.972)
  Pallas kernels: 58.1 us -> 56.4 us
    pallas_call x1, Pallas kernels: 58.1 us -> 56.4 us  [per_device(): pl.pallas_call(fused_kernel, out_shape=jax.ShapeDtypeStruct((TILE, HEADS...]
where the time goes in v7:
time: 58.4 us; the launch traced here: 58.2 us
  Pallas kernels  56.4 us (97%)
  local copies, waits for them, and re-layouts  1.87 us (3%)
    pallas_call x1, Pallas kernels, per_device(): pl.pallas_call(fused_kernel, out_shape=jax.ShapeDtypeStruct((TILE, HEADS...  56.4 us
    unnamed x1, local copies, waits for them, and re-layouts  1.87 us

profile of v7, /device:TPU:7, one launch (start us, length us, event | category | flops | bytes accessed | tf_op | source)
XLA Modules:
  0.0 58.2 jit_solution(7073079878278560225)
XLA Ops:
  0.0 56.4 %fused_attention.1 = bf16[64,4096]{1,0:T(8,128)(2,1)} custom-call(bf16[512,4096]{1,0:T(8,128)(2,1)} %q_hbm.1, bf16[512,2048]{1,0:T(8,128)(2,1)} %kv_hbm.1, s32[1,24]{1,0:T(1,128)} %verts_ref.1, s32[1,24]{1,0:T(1,128)} %slashes_ref.1, s32[1,192]{1,0:T(1,128)} %bitcast.1), custom_call_target="tpu_custom_call" | custom-call | tf_op jit(solution)/shard_map/fused_attention/pallas_call | solution.py:451
  56.4 1.9 %copy.7 = bf16[64,4096]{1,0:T(8,128)(2,1)} copy(bf16[64,4096]{1,0:T(8,128)(2,1)} %fused_attention.1) | data formatting | bytes 1048576

commit v8 on v7

--- a/solution.py
+++ b/solution.py
@@ -388,10 +388,13 @@
         elif n == 2:
             values.pass_on(-1)
             values.pass_on(1)
-        elif n == 3:
-            keys.drain()
+        elif n == 4:
+            values.far(0)
+            values.pass_on(2)
         elif n == 5:
-            values.ends()
+            values.far(-1)
+            values.far(1)
+            values.far(2)
             values.last()
 
     def out_copy(k, n):
@@ -412,7 +415,7 @@
             def _(batch):
                 tiles = [batch * BATCH + n for n in range(BATCH)]
                 score_tiles(k, tiles, first_tile, q_ref, k_buf, slots, bias_s, score_v, p_v, p_s, ell)
-                for n in (0, 2, 3, 5):
+                for n in (0, 2, 4, 5):
                     @pl.when(k * (TILES_LOCAL // BATCH) + batch == n)
                     def _():
                         gap(n)
@@ -424,6 +427,7 @@
             cols = pl.ds(pl.multiple_of((z * GROUP_HEADS + k) * HEAD_DIM, HEAD_DIM), HEAD_DIM)
             out_ref[:, cols] = out_buf[k, pl.ds(pl.multiple_of(z * TILE, TILE), TILE), :]
 
+    keys.drain()
     values.drain()
 
     @pl.when(z == owner)

time: 58.4 us -> 57.3 us (0.981)
  Pallas kernels: 56.4 us -> 55.3 us
    pallas_call x1, Pallas kernels: 56.4 us -> 55.3 us  [per_device(): pl.pallas_call(fused_kernel, out_shape=jax.ShapeDtypeStruct((TILE, HEADS...]
where the time goes in v8:
time: 57.3 us; the launch traced here: 57.1 us
  Pallas kernels  55.3 us (97%)
  local copies, waits for them, and re-layouts  1.87 us (3%)
    pallas_call x1, Pallas kernels, per_device(): pl.pallas_call(fused_kernel, out_shape=jax.ShapeDtypeStruct((TILE, HEADS...  55.3 us
    unnamed x1, local copies, waits for them, and re-layouts  1.87 us

profile of v8, /device:TPU:7, one launch (start us, length us, event | category | flops | bytes accessed | tf_op | source)
XLA Modules:
  0.0 57.1 jit_solution(14710863039145026243)
XLA Ops:
  0.0 55.3 %fused_attention.1 = bf16[64,4096]{1,0:T(8,128)(2,1)} custom-call(bf16[512,4096]{1,0:T(8,128)(2,1)} %q_hbm.1, bf16[512,2048]{1,0:T(8,128)(2,1)} %kv_hbm.1, s32[1,24]{1,0:T(1,128)} %verts_ref.1, s32[1,24]{1,0:T(1,128)} %slashes_ref.1, s32[1,192]{1,0:T(1,128)} %bitcast.1), custom_call_target="tpu_custom_call" | custom-call | tf_op jit(solution)/shard_map/fused_attention/pallas_call | solution.py:455
  55.3 1.9 %copy.7 = bf16[64,4096]{1,0:T(8,128)(2,1)} copy(bf16[64,4096]{1,0:T(8,128)(2,1)} %fused_attention.1) | data formatting | bytes 1048576

commit v9 on v8

--- a/solution.py
+++ b/solution.py
@@ -245,8 +245,9 @@
 
     def far(self, da):
         for half in (0, 1):
-            self.got(self.at(da, 2), half, lambda: self.need(self.me, self.at(da, 2)))
-        self.across(da, 2)
+            shard = self.at(da, 2)
+            self.got(shard, half, lambda: self.need(self.me, shard))
+            self.put(shard, half, self.sibling(self.me), lambda: self.need(self.me, self.at(da, 2)))
 
     def sends(self):
         self.near(-1, 1)
@@ -266,7 +267,8 @@
         for da in range(4):
             for db in range(4):
                 shard = self.sibling(self.at(da, db))
-                self.got(shard, None, lambda: self.need(self.me, shard))
+                for half in (0, 1) if da == 2 else (None,):
+                    self.got(shard, half, lambda: self.need(self.me, shard))
 
     def drain(self):
         for n, (half, cond) in enumerate(self.started):
@@ -275,7 +277,7 @@
                 self.copy(self.me, half, self.sibling(self.me), n).wait_send()
 
 
-N_SENDS = 49
+N_SENDS = 53
 N_SEQ = 32
 
 

time: 57.3 us -> 57.4 us (level)
  no operation moved by 1% of the time
where the time goes in v9:
time: 57.4 us; the launch traced here: 57.3 us
  Pallas kernels  55.4 us (97%)
  local copies, waits for them, and re-layouts  1.87 us (3%)
    pallas_call x1, Pallas kernels, per_device(): pl.pallas_call(fused_kernel, out_shape=jax.ShapeDtypeStruct((TILE, HEADS...  55.4 us
    unnamed x1, local copies, waits for them, and re-layouts  1.87 us

profile of v9, /device:TPU:7, one launch (start us, length us, event | category | flops | bytes accessed | tf_op | source)
XLA Modules:
  0.0 57.3 jit_solution(9345390652855130484)
XLA Ops:
  0.0 55.4 %fused_attention.1 = bf16[64,4096]{1,0:T(8,128)(2,1)} custom-call(bf16[512,4096]{1,0:T(8,128)(2,1)} %q_hbm.1, bf16[512,2048]{1,0:T(8,128)(2,1)} %kv_hbm.1, s32[1,24]{1,0:T(1,128)} %verts_ref.1, s32[1,24]{1,0:T(1,128)} %slashes_ref.1, s32[1,192]{1,0:T(1,128)} %bitcast.1), custom_call_target="tpu_custom_call" | custom-call | tf_op jit(solution)/shard_map/fused_attention/pallas_call | solution.py:457
  55.4 1.9 %copy.7 = bf16[64,4096]{1,0:T(8,128)(2,1)} copy(bf16[64,4096]{1,0:T(8,128)(2,1)} %fused_attention.1) | data formatting | bytes 1048576
